TPU v7x, 32 devices: a whole 2x2x4 slice. The times are simulated.
32 devices in a mesh: ctx: 4 (over y, x), fsdp: 8 (over z, core).
Axes of the slice: x: 2, y: 2, z: 4, core: 2. Of those that a mesh axis runs over, the one named last changes fastest.
Arguments:
- tokens: bfloat16 [8, 512, 1536], P('fsdp', 'ctx'), may hold values from -6 to 6
- document_starts: int32 [8, 8], P('fsdp'), may hold values from 0 to 512, as said below
- attention_weights: float32 [3584, 1536], P('fsdp'), may hold values from -0.4 to 0.4
- projection_bias: float32 [2048], P('fsdp'), may hold values from -3 to 3
- norm_gains: float32 [2, 1536], P(None, 'fsdp'), may hold values from 0.25 to 1.75
- hidden_weights: float32 [8960, 4608], P('fsdp'), may hold values from -0.15625 to 0.15625
- cotangent: bfloat16 [8, 512, 1536], P('fsdp', 'ctx'), may hold values from -6 to 6
Outputs:
- output: bfloat16 [8, 512, 1536], P('fsdp', 'ctx')
- input_gradient: float32 [8, 512, 1536], P('fsdp', 'ctx')
- attention_gradient: float32 [3584, 1536], P(('fsdp', 'ctx'))
- bias_gradient: float32 [2048], P(('fsdp', 'ctx'))
- gain_gradient: float32 [2, 1536], P(None, ('fsdp', 'ctx'))
- hidden_gradient: float32 [8960, 4608], P(('fsdp', 'ctx'))
Inputs may be any that keep to these rules, and one draw needn't show every extreme that they name: `document_starts`: each row rises strictly from 0 and then holds 512 as padding in its last slots; document j of a stream covers the positions from its entry up to the next entry.
All inputs are finite; a program needn't handle non-finite values.
Results may differ from a plain program's by a relative error of at most 0.024.
Values may be sent and summed in bfloat16 or wider, within the bound.
No kernel may reach another device: no remote copies, remote signals or barrier semaphores. Data moves between devices by JAX's collectives and lax.ppermute only.
A program may use at most 704 MiB of HBM per device.

v0:
```python
import jax
import jax.numpy as jnp
from jax import lax
from jax.sharding import PartitionSpec as P

HEADS = 12
KV_HEADS = 2
HEAD_DIM = 128


EPSILON = 1e-06
THETA = 10000.0
LOWEST = -1e30


def rope_tables(positions, width):
    half = width // 2
    frequency = THETA ** (-(jnp.arange(half, dtype=jnp.float32) * 2.0 / width))
    angle = positions.astype(jnp.float32)[:, None] * frequency[None, :]
    cosine = jnp.concatenate([jnp.cos(angle), jnp.cos(angle)], axis=1)
    sine = jnp.concatenate([jnp.sin(angle), jnp.sin(angle)], axis=1)
    return (cosine, sine)


def rotate(vectors, cosine, sine):
    half = vectors.shape[-1] // 2
    turned = jnp.concatenate([-vectors[..., half:], vectors[..., :half]], axis=-1)
    return vectors * cosine[:, None, :] + turned * sine[:, None, :]


def unrotate(gradient, cosine, sine):
    half = gradient.shape[-1] // 2
    moved = gradient * sine[:, None, :]
    return gradient * cosine[:, None, :] + jnp.concatenate(
        [moved[..., half:], -moved[..., :half]], axis=-1
    )


def segments(starts, positions):
    return jnp.sum((starts[None, :] <= positions[:, None]).astype(jnp.int32), axis=1) - 1


def inverse_rms(values):
    return lax.rsqrt(jnp.mean(values * values, axis=-1, keepdims=True) + EPSILON)


def norm_backward(inputs, scale, gain, back_normed):
    weighted = back_normed * gain
    back_inputs = scale * weighted - inputs * scale * scale * scale * jnp.mean(
        inputs * weighted, axis=-1, keepdims=True
    )
    return (back_inputs, jnp.sum(back_normed * inputs * scale, axis=0))


def hidden_values(normed, weights, width):
    gate_value = jnp.einsum(
        "td,fd->tf", normed, weights[:, :width], preferred_element_type=jnp.float32
    )
    up_value = jnp.einsum(
        "td,fd->tf", normed, weights[:, width : 2 * width], preferred_element_type=jnp.float32
    )
    sigmoid_gate = jax.nn.sigmoid(gate_value)
    silu_gate = gate_value * sigmoid_gate
    hidden = (silu_gate * up_value).astype(jnp.bfloat16)
    return (gate_value, up_value, sigmoid_gate, silu_gate, hidden)


def hidden_backward(upstream, weights, width, kept):
    gate_value, up_value, sigmoid_gate, silu_gate = kept
    back_hidden = jnp.einsum(
        "td,fd->tf", upstream, weights[:, 2 * width :], preferred_element_type=jnp.float32
    )
    back_up = (back_hidden * silu_gate).astype(jnp.bfloat16)
    back_gate = (
        back_hidden * up_value * sigmoid_gate * (1.0 + gate_value * (1.0 - sigmoid_gate))
    ).astype(jnp.bfloat16)
    return (back_gate, back_up)


def per_device(
    tokens,
    document_starts,
    attention_weights,
    projection_bias,
    norm_gains,
    hidden_weights,
    cotangent,
):
    rows = tokens.shape[1]
    width = tokens.shape[2]
    group = HEADS // KV_HEADS
    query_width = HEADS * HEAD_DIM
    key_width = KV_HEADS * HEAD_DIM
    projection_width = query_width + 2 * key_width
    scale = HEAD_DIM ** (-0.5)
    starts = document_starts[0]
    positions = lax.axis_index("ctx") * rows + jnp.arange(rows, dtype=jnp.int32)
    query_segment = segments(starts, positions)
    cosine, sine = rope_tables(positions, HEAD_DIM)
    block_weights, bias_all, gains_all = (
        lax.all_gather(attention_weights.astype(jnp.bfloat16), "fsdp", axis=0, tiled=True),
        lax.all_gather(projection_bias.astype(jnp.bfloat16), "fsdp", axis=0, tiled=True),
        lax.all_gather(norm_gains.astype(jnp.bfloat16), "fsdp", axis=1, tiled=True),
    )
    w_project = block_weights[:projection_width]
    w_output = block_weights[projection_width:]
    gain_one = gains_all[0].astype(jnp.float32)
    gain_two = gains_all[1].astype(jnp.float32)
    inputs = tokens[0].astype(jnp.float32)
    scale_one = inverse_rms(inputs)
    normed_one = (inputs * scale_one * gain_one).astype(jnp.bfloat16)
    projected = jnp.einsum(
        "td,rd->tr", normed_one, w_project, preferred_element_type=jnp.float32
    ) + bias_all.astype(jnp.float32)
    queries = rotate(
        projected[:, :query_width].reshape(rows, HEADS, HEAD_DIM), cosine, sine
    ).astype(jnp.bfloat16)
    queries = queries.reshape(rows, KV_HEADS, group, HEAD_DIM)
    keys = rotate(
        projected[:, query_width : query_width + key_width].reshape(rows, KV_HEADS, HEAD_DIM),
        cosine,
        sine,
    )
    keys = keys.astype(jnp.bfloat16).reshape(rows, key_width)
    values = projected[:, query_width + key_width :].astype(jnp.bfloat16)

    def allowed(first_key, count):
        key_positions = first_key + jnp.arange(count, dtype=jnp.int32)
        same_document = query_segment[:, None] == segments(starts, key_positions)[None, :]
        return same_document & (key_positions[None, :] <= positions[:, None])

    def masked_scores(key_block, mask):
        count = key_block.shape[0]
        raw = (
            jnp.einsum(
                "tkgd,skd->kgts",
                queries,
                key_block.reshape(count, KV_HEADS, HEAD_DIM),
                preferred_element_type=jnp.float32,
            )
            * scale
        )
        return jnp.where(mask, raw, -jnp.inf)

    initial = (
        jnp.full((KV_HEADS, group, rows), LOWEST, jnp.float32),
        jnp.zeros((KV_HEADS, group, rows), jnp.float32),
        jnp.zeros((KV_HEADS, group, rows, HEAD_DIM), jnp.float32),
    )
    key_block = lax.all_gather(keys, "ctx", axis=0, tiled=True)
    value_block = lax.all_gather(values, "ctx", axis=0, tiled=True)
    count = key_block.shape[0]
    mask = allowed(jnp.int32(0), count)

    def absorb_compute(current):
        top, total, accumulated = current
        scores = masked_scores(key_block, mask)
        new_top = jnp.maximum(top, jnp.max(scores, axis=-1))
        raised = jnp.exp(scores - new_top[..., None])
        mixed_block = jnp.einsum(
            "kgts,skd->kgtd",
            raised.astype(jnp.bfloat16),
            value_block.reshape(count, KV_HEADS, HEAD_DIM),
            preferred_element_type=jnp.float32,
        )
        return (new_top, jnp.sum(raised, axis=-1), mixed_block)

    top, total, accumulated = lax.cond(
        jnp.any(mask), absorb_compute, lambda current: current, initial
    )
    log_total = top + jnp.log(total)
    attention_out = accumulated / total[..., None]
    mixed_low = attention_out.transpose(2, 0, 1, 3).reshape(rows, query_width).astype(jnp.bfloat16)
    branch = jnp.einsum("tf,fd->td", mixed_low, w_output, preferred_element_type=jnp.float32)
    residual = inputs + branch
    scale_two = inverse_rms(residual)
    normed_two = (residual * scale_two * gain_two).astype(jnp.bfloat16)
    upstream = cotangent[0]
    hidden_low = hidden_weights.astype(jnp.bfloat16)
    hidden_all = lax.all_gather(hidden_low, "fsdp", axis=0, tiled=True)
    gate_value, up_value, sigmoid_gate, silu_gate, hidden = hidden_values(
        normed_two, hidden_all, width
    )
    lifted = jnp.dot(hidden, hidden_all[:, 2 * width :], preferred_element_type=jnp.float32)
    output = (residual + lifted).astype(jnp.bfloat16)
    back_gate, back_up = hidden_backward(
        upstream, hidden_all, width, (gate_value, up_value, sigmoid_gate, silu_gate)
    )
    back_normed_two = jnp.einsum(
        "tf,fd->td", back_gate, hidden_all[:, :width], preferred_element_type=jnp.float32
    )
    back_normed_two = back_normed_two + jnp.einsum(
        "tf,fd->td", back_up, hidden_all[:, width : 2 * width], preferred_element_type=jnp.float32
    )
    hidden_shard = lax.psum_scatter(
        jnp.concatenate(
            [
                jnp.einsum("tf,td->fd", back_gate, normed_two, preferred_element_type=jnp.float32),
                jnp.einsum("tf,td->fd", back_up, normed_two, preferred_element_type=jnp.float32),
                jnp.einsum("tf,td->fd", hidden, upstream, preferred_element_type=jnp.float32),
            ],
            axis=1,
        ).astype(jnp.bfloat16),
        "fsdp",
        scatter_dimension=0,
        tiled=True,
    ).astype(jnp.float32)
    back_residual_part, back_gain_two = norm_backward(
        residual, scale_two, gain_two, back_normed_two
    )
    back_residual = upstream.astype(jnp.float32) + back_residual_part
    back_branch = back_residual.astype(jnp.bfloat16)
    back_mixed = jnp.einsum(
        "td,fd->tf", back_branch, w_output, preferred_element_type=jnp.float32
    ).astype(jnp.bfloat16)
    back_mixed = back_mixed.reshape(rows, KV_HEADS, group, HEAD_DIM)
    back_output = jnp.einsum(
        "tf,td->fd", mixed_low, back_branch, preferred_element_type=jnp.float32
    )
    delta = jnp.sum(back_mixed.transpose(1, 2, 0, 3).astype(jnp.float32) * attention_out, axis=-1)
    keys_all, values_all = (
        lax.all_gather(keys, "ctx", axis=0, tiled=True),
        lax.all_gather(values, "ctx", axis=0, tiled=True),
    )
    total_keys = keys_all.shape[0]
    key_span = min(512, total_keys)

    def back_step(back_query, index):
        first_key = index * key_span
        key_block = lax.dynamic_slice_in_dim(keys_all, first_key, key_span, 0)
        value_block = lax.dynamic_slice_in_dim(values_all, first_key, key_span, 0)
        mask = allowed(first_key, key_span)

        def back_compute(current):
            scores = masked_scores(key_block, mask)
            probability = jnp.exp(scores - log_total[..., None])
            back_probability = jnp.einsum(
                "tkgd,skd->kgts",
                back_mixed,
                value_block.reshape(key_span, KV_HEADS, HEAD_DIM),
                preferred_element_type=jnp.float32,
            )
            back_scores = (probability * (back_probability - delta[..., None])).astype(jnp.bfloat16)
            key_heads = key_block.reshape(key_span, KV_HEADS, HEAD_DIM)
            current = (
                current
                + jnp.einsum(
                    "kgts,skd->kgtd", back_scores, key_heads, preferred_element_type=jnp.float32
                )
                * scale
            )
            back_keys = (
                jnp.einsum(
                    "kgts,tkgd->skd", back_scores, queries, preferred_element_type=jnp.float32
                )
                * scale
            )
            back_values = jnp.einsum(
                "kgts,tkgd->skd",
                probability.astype(jnp.bfloat16),
                back_mixed,
                preferred_element_type=jnp.float32,
            )
            return (
                current,
                back_keys.reshape(key_span, key_width),
                back_values.reshape(key_span, key_width),
            )

        def skip(current):
            empty = jnp.zeros((key_span, key_width), jnp.float32)
            return (current, empty, empty)

        back_query, back_keys, back_values = lax.cond(jnp.any(mask), back_compute, skip, back_query)
        return (back_query, (back_keys, back_values))

    back_query, (key_terms, value_terms) = lax.scan(
        back_step,
        jnp.zeros((KV_HEADS, group, rows, HEAD_DIM), jnp.float32),
        jnp.arange(total_keys // key_span, dtype=jnp.int32),
    )
    back_keys_own, back_values_own = (
        lax.psum_scatter(
            key_terms.reshape(total_keys, key_width).astype(jnp.bfloat16),
            "ctx",
            scatter_dimension=0,
            tiled=True,
        ).astype(jnp.float32),
        lax.psum_scatter(
            value_terms.reshape(total_keys, key_width).astype(jnp.bfloat16),
            "ctx",
            scatter_dimension=0,
            tiled=True,
        ).astype(jnp.float32),
    )
    back_query_heads = back_query.transpose(2, 0, 1, 3).reshape(rows, HEADS, HEAD_DIM)
    back_query_pre = unrotate(back_query_heads, cosine, sine).reshape(rows, query_width)
    back_key_pre = unrotate(back_keys_own.reshape(rows, KV_HEADS, HEAD_DIM), cosine, sine).reshape(
        rows, key_width
    )
    back_projected = jnp.concatenate(
        [back_query_pre, back_key_pre, back_values_own], axis=1
    ).astype(jnp.bfloat16)
    back_bias = jnp.sum(back_projected.astype(jnp.float32), axis=0)
    back_normed_one = jnp.einsum(
        "tr,rd->td", back_projected, w_project, preferred_element_type=jnp.float32
    )
    back_project = jnp.einsum(
        "tr,td->rd", back_projected, normed_one, preferred_element_type=jnp.float32
    )
    back_inputs_part, back_gain_one = norm_backward(inputs, scale_one, gain_one, back_normed_one)
    back_inputs = back_residual + back_inputs_part
    attention_term = jnp.concatenate([back_project, back_output], axis=0)
    gain_term = jnp.stack([back_gain_one, back_gain_two])
    attention_shard, bias_shard, gain_shard = (
        lax.psum_scatter(
            attention_term.astype(jnp.bfloat16), "fsdp", scatter_dimension=0, tiled=True
        ).astype(jnp.float32),
        lax.psum_scatter(
            back_bias.astype(jnp.bfloat16), "fsdp", scatter_dimension=0, tiled=True
        ).astype(jnp.float32),
        lax.psum_scatter(
            gain_term.astype(jnp.bfloat16), "fsdp", scatter_dimension=1, tiled=True
        ).astype(jnp.float32),
    )
    attention_shard, bias_shard, gain_shard, hidden_shard = (
        lax.psum_scatter(
            attention_shard.astype(jnp.bfloat16), "ctx", scatter_dimension=0, tiled=True
        ).astype(jnp.float32),
        lax.psum_scatter(
            bias_shard.astype(jnp.bfloat16), "ctx", scatter_dimension=0, tiled=True
        ).astype(jnp.float32),
        lax.psum_scatter(
            gain_shard.astype(jnp.bfloat16), "ctx", scatter_dimension=1, tiled=True
        ).astype(jnp.float32),
        lax.psum_scatter(
            hidden_shard.astype(jnp.bfloat16), "ctx", scatter_dimension=0, tiled=True
        ).astype(jnp.float32),
    )
    return (output[None], back_inputs[None], attention_shard, bias_shard, gain_shard, hidden_shard)


def solution(mesh):
    placed = (
        P("fsdp", "ctx", None),
        P("fsdp", None),
        P("fsdp", None),
        P("fsdp"),
        P(None, "fsdp"),
        P("fsdp", None),
        P("fsdp", "ctx", None),
    )
    return jax.shard_map(
        per_device,
        mesh=mesh,
        in_specs=placed,
        out_specs=(
            P("fsdp", "ctx", None),
            P("fsdp", "ctx", None),
            P(("fsdp", "ctx"), None),
            P(("fsdp", "ctx")),
            P(None, ("fsdp", "ctx")),
            P(("fsdp", "ctx"), None),
        ),
        check_vma=False,
    )
```

profile of v0, /device:TPU:17, one launch (start us, length us, event | category | flops | bytes accessed | tf_op | source)
XLA Modules:
  0.0 2253.1 jit_solution(5320807239175980417)
XLA Ops:
  7.2 3.0 convert_element_type.148
  10.3 12.2 convert_element_type.158
  23.2 11.0 all-gather
  34.3 8.2 all-gather.1
  44.8 69.3 %all-gather.5.cloned.1.call-done = bf16[3584,1536]{1,0:T(8,128)(2,1)} async-done(((bf16[448,1536]{1,0:T(8,128)(2,1)}), bf16[3584,1536]{1,0:T(8,128)(2,1)}) %all-gather.5.cloned.1.call-update) | async-done | bytes 11010064 | tf_op jit(solution)/shard_map/all_gather | solution.py:101
  114.1 4.9 fusion.60
  120.0 7.9 all_gather.23
  127.9 7.6 all_gather.24
  135.7 7.6 conditional.2
  139.0 2.0 fusion.1
  143.9 1.8 fusion.103
  145.7 3.7 multiply_reduce_fusion.3
  149.6 656.6 %all-gather.7.cloned.1.call-done = bf16[8960,4608]{1,0:T(8,128)(2,1)} async-done(((bf16[1120,4608]{1,0:T(8,128)(2,1)}), bf16[8960,4608]{1,0:T(8,128)(2,1)}) %all-gather.7.cloned.1.call-update) | async-done | bytes 82575376 | tf_op jit(solution)/shard_map/all_gather | solution.py:180
  806.1 15.8 fusion.30
  821.9 15.3 fusion.36
  837.2 17.9 multiply_convert_fusion.1
  855.1 11.8 fusion.34
  866.9 11.7 multiply_reduce_fusion.1
  879.6 4.3 fusion.63
  885.1 16.0 conditional.3
  886.5 1.7 reshape.121
  889.3 2.3 copy.107
  891.5 2.3 copy.106
  893.8 1.7 multiply_reduce_fusion
  896.1 1.6 fusion.19
  901.4 1.8 copy.109
  905.2 1.8 copy.136
  909.2 3.6 convolution_convert_fusion.4
  912.9 13.7 reduce-scatter.15.cloned.1.call-done
  929.0 25.1 %reduce-scatter.21.cloned.1.call-done = bf16[128,256]{1,0:T(8,128)(2,1)} async-done(((bf16[512,256]{1,0:T(8,128)(2,1)}), bf16[128,256]{1,0:T(8,128)(2,1)}) %reduce-scatter.21.cloned.1.call-update) | async-done | bytes 65552
  955.1 1.9 convolution_convert_fusion.3
  957.3 14.1 pad_maximum_fusion.1
  973.1 13.6 convolution_convert_fusion.2
  986.7 14.7 convolution_convert_fusion.1
  1001.5 12.9 convolution_convert_fusion
  1014.4 57.2 %pad_maximum_fusion = bf16[8960,4608]{0,1:T(8,128)(2,1)} fusion(bf16[8960,1536]{0,1:T(8,128)(2,1)} %convolution_convert_fusion, bf16[8960,1536]{0,1:T(8,128)(2,1)} %convolution_convert_fusion.1, bf16[8960,1536]{0,1:T(8,128)(2,1)} %convolution_convert_fusion.2), kind=kLoop, calls=%fused_computation.36 | loop fusion | flops 247726080 | bytes 165150720 | tf_op jit(solution)/shard_map/concatenate | solution.py:196
  1071.6 99.6 %copy.142 = bf16[8960,4608]{1,0:T(8,128)(2,1)} copy(bf16[8960,4608]{0,1:T(8,128)(2,1)} %pad_maximum_fusion) | data formatting | bytes 165150720
  1172.2 4.0 fusion.83
  1178.3 779.0 %reduce-scatter.25.cloned.1.call-done = bf16[1120,4608]{1,0:T(8,128)(2,1)} async-done(((bf16[8960,4608]{1,0:T(8,128)(2,1)}), bf16[1120,4608]{1,0:T(8,128)(2,1)}) %reduce-scatter.25.cloned.1.call-update) | async-done | bytes 10321936
  1957.3 15.2 copy.143
  1976.9 12.4 fusion.69
  1989.5 9.5 all-reduce
  2001.1 8.0 all-reduce.4
  2010.3 11.4 reduce-scatter.19.cloned.1.call-done
  2021.7 1.9 convert_element_type.171
  2023.6 209.6 %all-reduce.7.cloned.1.call-done = bf16[1120,4608]{0,1:T(8,128)(2,1)} async-done(((bf16[1120,4608]{0,1:T(8,128)(2,1)}), bf16[1120,4608]{0,1:T(8,128)(2,1)}) %all-reduce.7.cloned.1.call-update) | async-done | bytes 10321936
  2233.2 6.6 dynamic-slice_convert_fusion
  2239.8 6.5 copy.111
  (189 shorter events, 36.5 us)
Async XLA Ops:
  7.2 106.9 %all-gather.5.cloned.1.call-start = ((), (), s32[]{:S(2)}) async-start(), calls=%async_computation.6 | async-start | bytes 12386304 | tf_op jit(solution)/shard_map/all_gather | solution.py:101
  10.2 795.9 %all-gather.7.cloned.1.call-start = ((), (), s32[]{:S(2)}) async-start(), calls=%async_computation.7 | async-start | bytes 92897280 | tf_op jit(solution)/shard_map/all_gather | solution.py:180
  22.5 20.0 copy-start.40
  22.5 22.1 copy-start.2
  22.5 904.0 %reduce-scatter.15.cloned.1.call-start = ((), (), s32[]{:S(2)}) async-start(), calls=%async_computation.8 | async-start | bytes 327680 | tf_op jit(solution)/shard_map/reduce_scatter | solution.py:283
  43.4 92.3 %copy-start.20 = (pred[128,512]{0,1:T(8,128)(4,1)}, pred[128,512]{0,1:T(8,128)(4,1)S(1)}, u32[]{:S(2)}) copy-start(pred[128,512]{0,1:T(8,128)(4,1)S(1)} %get-tuple-element.211) | copy-start | bytes 196612
  44.3 91.2 %copy-start.19 = (f32[128,128]{0,1:T(8,128)}, f32[128,128]{0,1:T(8,128)S(1)}, u32[]{:S(2)}) copy-start(f32[128,128]{0,1:T(8,128)S(1)} %pad_maximum_fusion.6) | copy-start | bytes 196612
  44.4 75.3 %copy-start.26 = (f32[128,128]{1,0:T(8,128)}, f32[128,128]{1,0:T(8,128)S(1)}, u32[]{:S(2)}) copy-start(f32[128,128]{1,0:T(8,128)S(1)} %copy.100) | copy-start | bytes 196612
  44.5 91.1 %copy-start.18 = (f32[128,128]{0,1:T(8,128)}, f32[128,128]{0,1:T(8,128)S(1)}, u32[]{:S(2)}) copy-start(f32[128,128]{0,1:T(8,128)S(1)} %pad_maximum_fusion.5) | copy-start | bytes 196612
  44.6 910.4 %copy-start.29 = (f32[1536]{0:T(1024)}, f32[1536]{0:T(1024)S(1)}, u32[]{:S(2)}) copy-start(f32[1536]{0:T(1024)S(1)} %get-tuple-element.193) | copy-start | bytes 18436
  44.8 69.3 %copy-start.35 = (f32[128]{0:T(128)}, f32[128]{0:T(128)S(1)}, u32[]{:S(2)}) copy-start(f32[128]{0:T(128)S(1)} %add_rsqrt_fusion.1) | copy-start | bytes 1540
  120.0 15.7 copy-start.16
  143.9 662.2 %copy-start.12 = (bf16[1,128,1536]{2,1,0:T(8,128)(2,1)S(1)}, bf16[1,128,1536]{2,1,0:T(8,128)(2,1)}, u32[]{:S(2)}) copy-start(bf16[1,128,1536]{2,1,0:T(8,128)(2,1)} %param.17) | copy-start | bytes 1179652
  149.4 729.2 %copy-start.6 = (f32[128,1536]{1,0:T(8,128)}, f32[128,1536]{1,0:T(8,128)S(1)}, u32[]{:S(2)}) copy-start(f32[128,1536]{1,0:T(8,128)S(1)} %get-tuple-element.216) | copy-start | bytes 2359300
  149.4 717.5 %copy-start.38 = (f32[128]{0:T(128)}, f32[128]{0:T(128)S(1)}, u32[]{:S(2)}) copy-start(f32[128]{0:T(128)S(1)} %add_rsqrt_fusion) | copy-start | bytes 1540
  855.1 11.8 copy-start.9
  855.1 11.8 copy-start.10
  879.6 29.6 %copy-start = (f32[128,1536]{1,0:T(8,128)}, f32[128,1536]{1,0:T(8,128)S(1)}, u32[]{:S(2)}) copy-start(f32[128,1536]{1,0:T(8,128)S(1)} %subtract_add_fusion) | copy-start | bytes 2359300
  879.6 5.5 copy-start.32
  885.2 3.0 copy-start.14
  888.2 7.9 copy-start.33
  888.2 7.9 copy-start.21
  893.8 2.3 copy-start.15
  895.5 2.2 copy-start.28
  903.3 50.8 %reduce-scatter.21.cloned.1.call-start = ((), (), s32[]{:S(2)}) async-start(), calls=%async_computation.11 | async-start | bytes 327680
  909.2 45.9 %copy-start.4 = (bf16[128,1536]{0,1:T(8,128)(2,1)}, bf16[128,1536]{0,1:T(8,128)(2,1)S(1)}, u32[]{:S(2)}) copy-start(bf16[128,1536]{0,1:T(8,128)(2,1)S(1)} %fusion.87) | copy-start | bytes 1179652
  909.2 18.2 copy-start.27
  909.2 18.7 copy-start.17
  909.2 45.8 %copy-start.36 = (f32[128]{0:T(128)S(1)}, f32[128]{0:T(128)}, u32[]{:S(2)}) copy-start(f32[128]{0:T(128)} %copy-done.35) | copy-start | bytes 1540
  912.8 264.5 %reduce-scatter.17.cloned.1.call-start = ((), (), s32[]{:S(2)}) async-start(), calls=%async_computation.9 | async-start | bytes 12386304 | tf_op jit(solution)/shard_map/reduce_scatter | solution.py:316
  928.8 28.2 %slice-start = ((s8[4718592]{0:T(1024)(128)(4,1)}), s8[524288]{0:T(1024)(128)(4,1)S(1)}, s32[]{:S(2)}) async-start(s8[4718592]{0:T(1024)(128)(4,1)} %bitcast.146), calls=%async_computation.15 | async-start | bytes 1048576
  929.0 28.0 %copy-start.22 = (bf16[128,256]{0,1:T(8,128)(2,1)}, bf16[128,256]{0,1:T(8,128)(2,1)S(1)}, u32[]{:S(2)}) copy-start(bf16[128,256]{0,1:T(8,128)(2,1)S(1)} %copy.110) | copy-start | bytes 196612
  955.1 1.9 copy-start.24
  955.1 2.2 slice-start.1
  971.4 1.6 copy-start.11
  971.5 985.8 %reduce-scatter.25.cloned.1.call-start = ((), (), s32[]{:S(2)}) async-start(), calls=%async_computation.13 | async-start | bytes 92897280
  986.7 14.8 copy-start.8
  986.7 14.8 copy-start.13
  1171.1 1.1 copy-start.5
  1171.1 1.1 copy-start.23
  1171.1 1.1 copy-start.25
  1171.1 1.1 copy-start.30
  1171.2 829.1 %reduce-scatter.23.cloned.1.call-start = ((), (), s32[]{:S(2)}) async-start(), calls=%async_computation.12 | async-start | bytes 442368
  1177.3 844.5 %reduce-scatter.19.cloned.1.call-start = ((), (), s32[]{:S(2)}) async-start(), calls=%async_computation.10 | async-start | bytes 1720320 | tf_op jit(solution)/shard_map/reduce_scatter | solution.py:327
  1178.0 1055.2 %all-reduce.7.cloned.1.call-start = ((), (), s32[]{:S(2)}) async-start(), calls=%async_computation.14 | async-start | bytes 21233664
  1972.4 3.2 copy-start.42
  1972.4 4.4 copy-start.7
  1976.9 22.2 copy-start.1
  (7 other events, 5.4 us)
Sparse Core Ops, SparseCore 0:
  10.4 103.6 all-gather.4
  115.8 690.3 all-gather.6
  903.4 23.1 reduce-scatter.14
  930.0 24.0 reduce-scatter.20
  971.6 113.1 reduce-scatter.16
  1171.3 785.9 reduce-scatter.24
  1960.2 25.4 reduce-scatter.22
  1988.6 33.0 reduce-scatter.18
  2025.3 207.8 all-reduce.6
where the time goes:
time: 2260 us; the launch traced here: 2250 us
  waiting for transfers between devices  1770 us (78%)
  matrix products  156 us (7%)
  local copies, waits for them, and re-layouts  146 us (6%)
  other arithmetic  114 us (5%)
  blocking collectives  52 us (2%)
    unnamed x13, waiting for transfers between devices  1010 us
    all_gather x1, waiting for transfers between devices, per_device(): hidden_all = lax.all_gather(hidden_low, 'fsdp', axis=0, tiled=True)  657 us
    unnamed x94, local copies, waits for them, and re-layouts  132 us
    all_gather x1, waiting for transfers between devices, per_device(): lax.all_gather(attention_weights.astype(jnp.bfloat16), 'fsdp', axis=0, ti...  69.3 us
    concatenate x1, other arithmetic, per_device(): jnp.concatenate([jnp.einsum('tf,td->fd', back_gate, normed_two, preferred...  57.2 us
  transfers between devices with their start and end apart: 9, of which 7 were waited for; matrix products, arithmetic and copies ran while one was open for 13% of the time, Pallas kernels for 0%

commit v1 on v0

--- a/solution.py
+++ b/solution.py
@@ -106,6 +106,9 @@
     w_output = block_weights[projection_width:]
     gain_one = gains_all[0].astype(jnp.float32)
     gain_two = gains_all[1].astype(jnp.float32)
+    upstream = cotangent[0]
+    upstream_all = lax.all_gather(upstream, "fsdp", axis=0, tiled=True)
+    hidden_low = hidden_weights.astype(jnp.bfloat16)
     inputs = tokens[0].astype(jnp.float32)
     scale_one = inverse_rms(inputs)
     normed_one = (inputs * scale_one * gain_one).astype(jnp.bfloat16)
@@ -175,36 +178,34 @@
     residual = inputs + branch
     scale_two = inverse_rms(residual)
     normed_two = (residual * scale_two * gain_two).astype(jnp.bfloat16)
-    upstream = cotangent[0]
-    hidden_low = hidden_weights.astype(jnp.bfloat16)
-    hidden_all = lax.all_gather(hidden_low, "fsdp", axis=0, tiled=True)
+    normed_all = lax.all_gather(normed_two, "fsdp", axis=0, tiled=True)
     gate_value, up_value, sigmoid_gate, silu_gate, hidden = hidden_values(
-        normed_two, hidden_all, width
-    )
-    lifted = jnp.dot(hidden, hidden_all[:, 2 * width :], preferred_element_type=jnp.float32)
+        normed_all, hidden_low, width
+    )
+    back_gate, back_up = hidden_backward(
+        upstream_all, hidden_low, width, (gate_value, up_value, sigmoid_gate, silu_gate)
+    )
+    back_normed_part = jnp.einsum(
+        "tf,fd->td", back_gate, hidden_low[:, :width], preferred_element_type=jnp.float32
+    ) + jnp.einsum(
+        "tf,fd->td", back_up, hidden_low[:, width : 2 * width], preferred_element_type=jnp.float32
+    )
+    back_normed_two = lax.psum_scatter(
+        back_normed_part.astype(jnp.bfloat16), "fsdp", scatter_dimension=0, tiled=True
+    ).astype(jnp.float32)
+    lifted_part = jnp.dot(hidden, hidden_low[:, 2 * width :], preferred_element_type=jnp.float32)
+    lifted = lax.psum_scatter(
+        lifted_part.astype(jnp.bfloat16), "fsdp", scatter_dimension=0, tiled=True
+    ).astype(jnp.float32)
     output = (residual + lifted).astype(jnp.bfloat16)
-    back_gate, back_up = hidden_backward(
-        upstream, hidden_all, width, (gate_value, up_value, sigmoid_gate, silu_gate)
-    )
-    back_normed_two = jnp.einsum(
-        "tf,fd->td", back_gate, hidden_all[:, :width], preferred_element_type=jnp.float32
-    )
-    back_normed_two = back_normed_two + jnp.einsum(
-        "tf,fd->td", back_up, hidden_all[:, width : 2 * width], preferred_element_type=jnp.float32
-    )
-    hidden_shard = lax.psum_scatter(
-        jnp.concatenate(
-            [
-                jnp.einsum("tf,td->fd", back_gate, normed_two, preferred_element_type=jnp.float32),
-                jnp.einsum("tf,td->fd", back_up, normed_two, preferred_element_type=jnp.float32),
-                jnp.einsum("tf,td->fd", hidden, upstream, preferred_element_type=jnp.float32),
-            ],
-            axis=1,
-        ).astype(jnp.bfloat16),
-        "fsdp",
-        scatter_dimension=0,
-        tiled=True,
-    ).astype(jnp.float32)
+    hidden_term = jnp.concatenate(
+        [
+            jnp.einsum("tf,td->fd", back_gate, normed_all, preferred_element_type=jnp.float32),
+            jnp.einsum("tf,td->fd", back_up, normed_all, preferred_element_type=jnp.float32),
+            jnp.einsum("tf,td->fd", hidden, upstream_all, preferred_element_type=jnp.float32),
+        ],
+        axis=1,
+    ).astype(jnp.bfloat16)
     back_residual_part, back_gain_two = norm_backward(
         residual, scale_two, gain_two, back_normed_two
     )
@@ -334,7 +335,7 @@
             gain_shard.astype(jnp.bfloat16), "ctx", scatter_dimension=1, tiled=True
         ).astype(jnp.float32),
         lax.psum_scatter(
-            hidden_shard.astype(jnp.bfloat16), "ctx", scatter_dimension=0, tiled=True
+            hidden_term, "ctx", scatter_dimension=0, tiled=True
         ).astype(jnp.float32),
     )
     return (output[None], back_inputs[None], attention_shard, bias_shard, gain_shard, hidden_shard)

time: 2260 us -> 736 us (0.33)
  waiting for transfers between devices: 1770 us -> 466 us
  local copies, waits for them, and re-layouts: 146 us -> 19 us
  matrix products: 156 us -> 106 us
  other arithmetic: 114 us -> 64.1 us
    unnamed x13 -> x14, waiting for transfers between devices: 1010 us -> 140 us
    all_gather x1 -> x2, waiting for transfers between devices: 657 us -> 49.4 us  [the longest x1 27.3 us: per_device(): normed_all = lax.all_gather(normed_two, 'fsdp', axis=0, tiled=True)]
    unnamed x94 -> x77, local copies, waits for them, and re-layouts: 132 us -> 7.67 us
    reduce_scatter x1, waiting for transfers between devices: 0.02 us -> 82.4 us  [per_device(): lax.psum_scatter(attention_term.astype(jnp.bfloat16), 'fsdp', scatter_dim...]
    reduce_scatter x0 -> x2, waiting for transfers between devices: none -> 69.1 us  [the longest x1 39.8 us: per_device(): lax.psum_scatter(lifted_part.astype(jnp.bfloat16), 'fsdp', scatter_dimens...]
    concatenate x1, other arithmetic: 57.2 us -> 9.58 us  [per_device(): jnp.concatenate([jnp.einsum('tf,td->fd', back_gate, normed_all, preferred...]
    dot_general x6, matrix products: 77.1 us -> 43.6 us  [the longest x1 8.6 us: per_device(): jnp.dot(hidden, hidden_low[:, 2 * width:], preferred_element_type=jnp.flo...]
  transfers between devices with their start and end apart: 9 -> 11, of which waited for: 7 -> 11; matrix products, arithmetic and copies ran while one was open for 13% -> 12% of each run, Pallas kernels for 0% -> 0%
where the time goes in v1:
time: 736 us; the launch traced here: 728 us
  waiting for transfers between devices  466 us (63%)
  matrix products  106 us (14%)
  other arithmetic  64.1 us (9%)
  blocking collectives  53.9 us (7%)
  local copies, waits for them, and re-layouts  19 us (3%)
  between operations  17.4 us (2%)
    unnamed x14, waiting for transfers between devices  140 us
    reduce_scatter x1, waiting for transfers between devices, per_device(): lax.psum_scatter(attention_term.astype(jnp.bfloat16), 'fsdp', scatter_dim...  82.4 us
    all_gather x1, waiting for transfers between devices, per_device(): lax.all_gather(attention_weights.astype(jnp.bfloat16), 'fsdp', axis=0, ti...  79.1 us
    reduce_scatter x1, waiting for transfers between devices, per_device(): lax.psum_scatter(lifted_part.astype(jnp.bfloat16), 'fsdp', scatter_dimens...  39.8 us
    reduce_scatter x1, waiting for transfers between devices, per_device(): lax.psum_scatter(back_normed_part.astype(jnp.bfloat16), 'fsdp', scatter_d...  29.4 us
    reduce_scatter x1, waiting for transfers between devices, per_device(): lax.psum_scatter(attention_shard.astype(jnp.bfloat16), 'ctx', scatter_dim...  28 us
    all_gather x1, waiting for transfers between devices, per_device(): normed_all = lax.all_gather(normed_two, 'fsdp', axis=0, tiled=True)  27.3 us
    all_gather x1, waiting for transfers between devices, per_device(): upstream_all = lax.all_gather(upstream, 'fsdp', axis=0, tiled=True)  22.1 us
  transfers between devices with their start and end apart: 11, of which 11 were waited for; matrix products, arithmetic and copies ran while one was open for 12% of the time, Pallas kernels for 0%

profile of v1, /device:TPU:17, one launch (start us, length us, event | category | flops | bytes accessed | tf_op | source)
XLA Modules:
  0.0 727.5 jit_solution(12311683630199250264)
XLA Ops:
  7.3 3.0 convert_element_type.158
  12.7 9.5 %all-gather.2 = bf16[8,1,256]{2,1,0:T(2,128)(2,1)S(1)} all-gather(bf16[1,1,256]{2,1,0:T(2,128)(2,1)S(1)} %reshape.145), channel_id=1, replica_groups=mesh['ctx'=4,'fsdp'=8] {'fsdp'}, dimensions={0}, use_global_device_ids=true | all-gather | bytes 4608 | tf_op jit(solution)/shard_map/all_gather | solution.py:102
  22.3 12.0 %all-gather.1 = bf16[8,192,2]{1,2,0:T(2,128)(2,1)S(1)} all-gather(bf16[1,192,2]{1,2,0:T(2,128)(2,1)S(1)} %convert_bitcast_fusion.1), channel_id=1, replica_groups=mesh['ctx'=4,'fsdp'=8] {'fsdp'}, dimensions={0}, use_global_device_ids=true | all-gather | bytes 6912 | tf_op jit(solution)/shard_map/all_gather | solution.py:103
  35.0 79.1 %all-gather.7.cloned.1.call-done = bf16[3584,1536]{1,0:T(8,128)(2,1)} async-done(((bf16[448,1536]{1,0:T(8,128)(2,1)}), bf16[3584,1536]{1,0:T(8,128)(2,1)}) %all-gather.7.cloned.1.call-update) | async-done | bytes 11010064 | tf_op jit(solution)/shard_map/all_gather | solution.py:101
  114.1 4.9 fusion.54
  120.4 6.9 all_gather.26
  127.7 7.9 %all_gather.27 = bf16[512,256]{1,0:T(8,128)(2,1)} all-gather(bf16[128,256]{1,0:T(8,128)(2,1)S(1)} %slice.132), channel_id=1, replica_groups=mesh['ctx'=4,'fsdp'=8] {'ctx'}, dimensions={0}, use_global_device_ids=true | all-gather | bytes 327680 | tf_op jit(solution)/shard_map/all_gather | solution.py:154
  135.7 10.6 %conditional.2 = (f32[2,6,128]{2,1,0:T(8,128)}, f32[2,6,128]{2,1,0:T(8,128)}, f32[2,6,128]{2,1,0:T(8,128)}, f32[2,6,128,128]{2,3,1,0:T(8,128)}) conditional(s32[]{:T(128)} %convert_element_type.155, () %tuple.29, (pred[128,512]{0,1:T(8,128)(4,1)}, bf16[512,256]{1,0:T(8,128)(2,1)S(1)}, bf16[128,2,6,128]{0,3,2,1:T(8,128)(2,1)S(1)}, ...), branch_computations={%region_4.0_spmd, %region_5.8_spmd} | conditional | flops 411302400 | bytes 12697660 | solution.py:171
  138.7 1.9 fusion.1
  143.6 2.7 fusion.3
  146.4 2.2 fusion.96
  148.5 3.3 multiply_reduce_fusion.1
  153.7 12.0 %convert_element_type.168 = bf16[1120,4608]{1,0:T(8,128)(2,1)} convert(f32[1120,4608]{1,0:T(8,128)} %param.16) | non-fusion elementwise | flops 5160960 | bytes 30965760 | tf_op jit(solution)/shard_map/convert_element_type | solution.py:111
  165.7 27.3 %all-gather.9.cloned.1.call-done = bf16[1024,1536]{1,0:T(8,128)(2,1)} async-done(((bf16[128,1536]{1,0:T(8,128)(2,1)}), bf16[1024,1536]{1,0:T(8,128)(2,1)}) %all-gather.9.cloned.1.call-update) | async-done | bytes 3145744 | tf_op jit(solution)/shard_map/all_gather | solution.py:181
  193.0 9.0 %fusion.49 = f32[1024,1120]{0,1:T(8,128)} fusion(bf16[1024,1536]{1,0:T(8,128)(2,1)} %all-gather.9.cloned.1.call-done, bf16[1120,4608]{1,0:T(8,128)(2,1)} %convert_element_type.168), kind=kOutput, calls=%fused_computation.68 | convolution fusion | flops 3523215360 | bytes 11173888 | tf_op jit(solution)/shard_map/td,fd->tf/dot_general | solution.py:56
  202.0 7.7 %fusion.45 = f32[1024,1120]{0,1:T(8,128)} fusion(bf16[1024,1536]{1,0:T(8,128)(2,1)S(1)} %copy-done.25, bf16[1120,4608]{1,0:T(8,128)(2,1)} %convert_element_type.168), kind=kOutput, calls=%fused_computation.64 | convolution fusion | flops 3523215360 | bytes 11173888 | tf_op jit(solution)/shard_map/td,fd->tf/dot_general | solution.py:59
  209.8 22.1 %all-gather.11.cloned.1.call-done = bf16[1,1024,1536]{2,1,0:T(8,128)(2,1)} async-done(((bf16[1,128,1536]{2,1,0:T(8,128)(2,1)}), bf16[1,1024,1536]{2,1,0:T(8,128)(2,1)}) %all-gather.11.cloned.1.call-update) | async-done | bytes 3145744 | tf_op jit(solution)/shard_map/all_gather | solution.py:110
  231.9 12.4 %multiply_convert_fusion = (bf16[1024,1120]{0,1:T(8,128)(2,1)S(1)}, bf16[1024,1120]{0,1:T(8,128)(2,1)S(1)}, bf16[1024,1120]{0,1:T(8,128)(2,1)}) fusion(f32[1024,1120]{0,1:T(8,128)} %fusion.49, f32[1024,1120]{0,1:T(8,128)} %fusion.45, bf16[1120,4608]{1,0:T(8,128)(2,1)} %convert_element_type.168, bf16[1,1024,1536]{2,1,0:T(8,128)(2,1)} %all-gather.11.cloned.1.call-done), kind=kOutput, calls=%fused_computation.48 | convolution fusion | flops 3540418560 | bytes 22642688 | tf_op jit(solution)/shard_map/td,fd->tf/dot_general | solution.py:70
  244.2 8.1 %fusion.47 = f32[1024,1536]{1,0:T(8,128)S(1)} fusion(bf16[1024,1120]{0,1:T(8,128)(2,1)S(1)} %get-tuple-element.177, bf16[1120,4608]{1,0:T(8,128)(2,1)} %convert_element_type.168), kind=kOutput, calls=%fused_computation.66 | convolution fusion | flops 3523215360 | bytes 12025856 | tf_op jit(solution)/shard_map/tf,fd->td/dot_general | solution.py:188
  252.3 8.2 %add_convert_fusion = bf16[1024,1536]{1,0:T(8,128)(2,1)} fusion(f32[1024,1536]{1,0:T(8,128)S(1)} %fusion.47, bf16[1024,1120]{0,1:T(8,128)(2,1)S(1)} %get-tuple-element.176, bf16[1120,4608]{1,0:T(8,128)(2,1)} %convert_element_type.168), kind=kOutput, calls=%fused_computation.43 | convolution fusion | flops 3526361088 | bytes 15171584 | tf_op jit(solution)/shard_map/tf,fd->td/dot_general | solution.py:190
  260.6 8.6 %convolution_convert_fusion.5 = bf16[1024,1536]{1,0:T(8,128)(2,1)} fusion(bf16[1024,1120]{0,1:T(8,128)(2,1)} %get-tuple-element.178, bf16[1120,4608]{1,0:T(8,128)(2,1)} %convert_element_type.168), kind=kOutput, calls=%fused_computation.57 | convolution fusion | flops 3524788224 | bytes 8880128 | tf_op jit(solution)/shard_map/dot_general | solution.py:196
  269.3 29.4 %reduce-scatter.18.cloned.1.call-done = bf16[128,1536]{1,0:T(8,128)(2,1)} async-done(((bf16[1024,1536]{1,0:T(8,128)(2,1)}), bf16[128,1536]{1,0:T(8,128)(2,1)}) %reduce-scatter.18.cloned.1.call-update) | async-done | bytes 393232 | tf_op jit(solution)/shard_map/reduce_scatter | solution.py:193
  298.7 1.8 fusion.74
  300.5 39.8 %reduce-scatter.16.cloned.1.call-done = bf16[128,1536]{1,0:T(8,128)(2,1)} async-done(((bf16[1024,1536]{1,0:T(8,128)(2,1)}), bf16[128,1536]{1,0:T(8,128)(2,1)}) %reduce-scatter.16.cloned.1.call-update) | async-done | bytes 393232 | tf_op jit(solution)/shard_map/reduce_scatter | solution.py:197
  340.3 2.2 fusion.71
  342.5 4.0 fusion.57
  347.6 15.8 %conditional.3 = (f32[2,6,128,128]{3,2,1,0:T(8,128)S(1)}, bf16[512,256]{0,1:T(8,128)(2,1)}, bf16[512,256]{0,1:T(8,128)(2,1)}) conditional(s32[]{:T(128)} %convert_element_type.155, f32[2,6,128,128]{3,2,1,0:T(8,128)S(1)} %broadcast.137, (pred[128,512]{0,1:T(8,128)(4,1)S(1)}, bf16[512,256]{1,0:T(8,128)(2,1)S(1)}, ...), branch_computations={%region_12.13_spmd, %region_13.0_spmd} | conditional | flops 1015545856 | bytes 40806536 | solution.py:275
  348.4 3.2 fusion.26
  356.4 3.0 fusion.15
  363.3 1.8 copy.106
  366.0 1.8 copy.132
  368.0 3.6 convolution_convert_fusion.4
  371.7 18.3 %reduce-scatter.20.cloned.1.call-done = bf16[128,256]{1,0:T(8,128)(2,1)} async-done(((bf16[512,256]{1,0:T(8,128)(2,1)}), bf16[128,256]{1,0:T(8,128)(2,1)}) %reduce-scatter.20.cloned.1.call-update) | async-done | bytes 65552 | tf_op jit(solution)/shard_map/reduce_scatter | solution.py:284
  392.4 25.3 %reduce-scatter.26.cloned.1.call-done = bf16[128,256]{1,0:T(8,128)(2,1)} async-done(((bf16[512,256]{1,0:T(8,128)(2,1)}), bf16[128,256]{1,0:T(8,128)(2,1)}) %reduce-scatter.26.cloned.1.call-update) | async-done | bytes 65552
  418.7 1.9 convolution_convert_fusion.3
  420.9 14.2 %pad_maximum_fusion = bf16[3584,1536]{1,0:T(8,128)(2,1)} fusion(bf16[1536,1536]{1,0:T(8,128)(2,1)S(1)} %bitcast.148, bf16[2048,1536]{1,0:T(8,128)(2,1)S(1)} %convolution_convert_fusion.3), kind=kLoop, calls=%fused_computation.36 | loop fusion | flops 22020096 | bytes 22020096 | tf_op jit(solution)/shard_map/concatenate | solution.py:314
  435.4 8.3 %convolution_convert_fusion = bf16[1120,1536]{1,0:T(8,128)(2,1)} fusion(bf16[1024,1120]{0,1:T(8,128)(2,1)} %get-tuple-element.178, bf16[1,1024,1536]{2,1,0:T(8,128)(2,1)} %all-gather.11.cloned.1.call-done), kind=kOutput, calls=%fused_computation.38 | convolution fusion | flops 3524935680 | bytes 8880128 | tf_op jit(solution)/shard_map/tf,td->fd/dot_general | solution.py:205
  443.7 5.3 convolution_convert_fusion.1
  448.9 5.2 convolution_convert_fusion.2
  456.5 9.6 %pad_maximum_fusion.1 = bf16[1120,4608]{1,0:T(8,128)(2,1)} fusion(bf16[1120,1536]{1,0:T(8,128)(2,1)} %convolution_convert_fusion, bf16[1120,1536]{1,0:T(8,128)(2,1)} %convolution_convert_fusion.1, bf16[1120,1536]{1,0:T(8,128)(2,1)} %convolution_convert_fusion.2), kind=kLoop, calls=%fused_computation.37 | loop fusion | flops 30965760 | bytes 20643840 | tf_op jit(solution)/shard_map/concatenate | solution.py:201
  466.1 82.4 %reduce-scatter.22.cloned.1.call-done = bf16[448,1536]{1,0:T(8,128)(2,1)} async-done(((bf16[3584,1536]{1,0:T(8,128)(2,1)}), bf16[448,1536]{1,0:T(8,128)(2,1)}) %reduce-scatter.22.cloned.1.call-update) | async-done | bytes 1376272 | tf_op jit(solution)/shard_map/reduce_scatter | solution.py:317
  551.8 9.5 %all-reduce = bf16[2048]{0:T(1024)(128)(2,1)S(1)} all-reduce(bf16[2048]{0:T(1024)(128)(2,1)S(1)} %fusion.94), channel_id=9, replica_groups=mesh['ctx'=4,'fsdp'=8] {'fsdp'}, use_global_device_ids=true, to_apply=%region_21.22.clone | all-reduce | flops 2048 | bytes 8192
  562.6 14.1 %reduce-scatter.28.cloned.1.call-done = bf16[192,2]{1,0:T(8,128)(2,1)} async-done(((bf16[1536,2]{1,0:T(8,128)(2,1)}), bf16[192,2]{1,0:T(8,128)(2,1)}) %reduce-scatter.28.cloned.1.call-update) | async-done | bytes 784
  577.6 8.0 %all-reduce.4 = (bf16[256]{0:T(256)(128)(2,1)S(1)}, bf16[2,192]{1,0:T(2,128)(2,1)S(1)}) all-reduce(bf16[256]{0:T(256)(128)(2,1)S(1)} %dynamic-slice.1, bf16[2,192]{1,0:T(2,128)(2,1)S(1)} %copy.135), channel_id=10, replica_groups=mesh['ctx'=4,'fsdp'=8] {'ctx'}, use_global_device_ids=true, to_apply=%region_22.23.clone | all-reduce | flops 640 | bytes 2560
  586.8 99.4 %reduce-scatter.30.cloned.1.call-done = bf16[280,4608]{1,0:T(8,128)(2,1)} async-done(((bf16[1120,4608]{1,0:T(8,128)(2,1)}), bf16[280,4608]{1,0:T(8,128)(2,1)}) %reduce-scatter.30.cloned.1.call-update) | async-done | bytes 2580496
  686.2 4.7 convert_element_type.188
  690.9 28.0 %reduce-scatter.24.cloned.1.call-done = bf16[112,1536]{1,0:T(8,128)(2,1)} async-done(((bf16[448,1536]{1,0:T(8,128)(2,1)}), bf16[112,1536]{1,0:T(8,128)(2,1)}) %reduce-scatter.24.cloned.1.call-update) | async-done | bytes 344080 | tf_op jit(solution)/shard_map/reduce_scatter | solution.py:328
  718.9 1.9 convert_element_type.185
  (180 shorter events, 34.7 us)
Async XLA Ops:
  7.2 3.2 copy-start.24
  7.2 5.5 copy-start.27
  7.2 15.1 %copy-start.23 = (f32[2,192]{1,0:T(2,128)S(1)}, f32[2,192]{1,0:T(2,128)}, u32[]{:S(2)}) copy-start(f32[2,192]{1,0:T(2,128)} %param.15) | copy-start | bytes 4612
  7.2 27.7 %copy-start = (bf16[1,128,1536]{2,1,0:T(8,128)(2,1)S(1)}, bf16[1,128,1536]{2,1,0:T(8,128)(2,1)}, u32[]{:S(2)}) copy-start(bf16[1,128,1536]{2,1,0:T(8,128)(2,1)} %param.11) | copy-start | bytes 1179652
  7.2 106.9 %all-gather.7.cloned.1.call-start = ((), (), s32[]{:S(2)}) async-start(), calls=%async_computation.8 | async-start | bytes 12386304 | tf_op jit(solution)/shard_map/all_gather | solution.py:101
  10.3 182.7 %all-gather.9.cloned.1.call-start = ((), (), s32[]{:S(2)}) async-start(), calls=%async_computation.9 | async-start | bytes 3538944 | tf_op jit(solution)/shard_map/all_gather | solution.py:181
  34.6 101.0 %copy-start.14 = (f32[128,128]{0,1:T(8,128)}, f32[128,128]{0,1:T(8,128)S(1)}, u32[]{:S(2)}) copy-start(f32[128,128]{0,1:T(8,128)S(1)} %pad_maximum_fusion.6) | copy-start | bytes 196612
  34.7 84.8 %copy-start.18 = (f32[128,128]{1,0:T(8,128)}, f32[128,128]{1,0:T(8,128)S(1)}, u32[]{:S(2)}) copy-start(f32[128,128]{1,0:T(8,128)S(1)} %copy.97) | copy-start | bytes 196612
  34.7 100.9 %copy-start.12 = (f32[128,128]{0,1:T(8,128)}, f32[128,128]{0,1:T(8,128)S(1)}, u32[]{:S(2)}) copy-start(f32[128,128]{0,1:T(8,128)S(1)} %pad_maximum_fusion.5) | copy-start | bytes 196612
  35.0 84.0 %copy-start.21 = (f32[128]{0:T(128)}, f32[128]{0:T(128)S(1)}, u32[]{:S(2)}) copy-start(f32[128]{0:T(128)S(1)} %add_rsqrt_fusion.1) | copy-start | bytes 1540
  127.3 8.4 %copy-start.3 = (bf16[512,256]{1,0:T(8,128)(2,1)}, bf16[512,256]{1,0:T(8,128)(2,1)S(1)}, u32[]{:S(2)}) copy-start(bf16[512,256]{1,0:T(8,128)(2,1)S(1)} %all_gather.26) | copy-start | bytes 786436
  136.5 2.2 copy-start.17
  152.8 79.1 %all-gather.11.cloned.1.call-start = ((), (), s32[]{:S(2)}) async-start(), calls=%async_computation.15 | async-start | bytes 3538944 | tf_op jit(solution)/shard_map/all_gather | solution.py:110
  153.5 145.2 %reduce-scatter.18.cloned.1.call-start = ((), (), s32[]{:S(2)}) async-start(), calls=%async_computation.11 | async-start | bytes 3538944 | tf_op jit(solution)/shard_map/reduce_scatter | solution.py:193
  193.0 9.0 %copy-start.25 = (bf16[1024,1536]{1,0:T(8,128)(2,1)S(1)}, bf16[1024,1536]{1,0:T(8,128)(2,1)}, u32[]{:S(2)}) copy-start(bf16[1024,1536]{1,0:T(8,128)(2,1)} %all-gather.9.cloned.1.call-done) | copy-start | bytes 9437188
  244.2 8.1 %copy-start.32 = (bf16[1024,1120]{0,1:T(8,128)(2,1)}, bf16[1024,1120]{0,1:T(8,128)(2,1)S(1)}, u32[]{:S(2)}) copy-start(bf16[1024,1120]{0,1:T(8,128)(2,1)S(1)} %get-tuple-element.177) | copy-start | bytes 6881284
  244.2 8.1 %copy-start.30 = (bf16[1024,1120]{0,1:T(8,128)(2,1)}, bf16[1024,1120]{0,1:T(8,128)(2,1)S(1)}, u32[]{:S(2)}) copy-start(bf16[1024,1120]{0,1:T(8,128)(2,1)S(1)} %get-tuple-element.176) | copy-start | bytes 6881284
  260.5 79.7 %reduce-scatter.16.cloned.1.call-start = ((), (), s32[]{:S(2)}) async-start(), calls=%async_computation.10 | async-start | bytes 3538944 | tf_op jit(solution)/shard_map/reduce_scatter | solution.py:197
  269.2 71.1 %copy-start.9 = (bf16[1,128,1536]{2,1,0:T(8,128)(2,1)S(1)}, bf16[1,128,1536]{2,1,0:T(8,128)(2,1)}, u32[]{:S(2)}) copy-start(bf16[1,128,1536]{2,1,0:T(8,128)(2,1)} %param.17) | copy-start | bytes 1179652
  269.2 120.8 %reduce-scatter.20.cloned.1.call-start = ((), (), s32[]{:S(2)}) async-start(), calls=%async_computation.12 | async-start | bytes 327680 | tf_op jit(solution)/shard_map/reduce_scatter | solution.py:284
  342.5 5.1 copy-start.4
  342.5 5.1 copy-start.16
  347.6 18.3 %copy-start.15 = (f32[128,128]{0,1:T(8,128)S(1)}, f32[128,128]{0,1:T(8,128)}, u32[]{:S(2)}) copy-start(f32[128,128]{0,1:T(8,128)} %copy-done.14) | copy-start | bytes 196612
  351.5 4.8 copy-start.5
  356.4 3.0 copy-start.6
  359.4 2.3 copy-start.2
  359.4 2.3 copy-start.8
  365.1 52.5 %reduce-scatter.26.cloned.1.call-start = ((), (), s32[]{:S(2)}) async-start(), calls=%async_computation.16 | async-start | bytes 327680
  365.6 2.3 copy-start.13
  368.0 22.9 %copy-start.19 = (f32[128,128]{1,0:T(8,128)S(1)}, f32[128,128]{1,0:T(8,128)}, u32[]{:S(2)}) copy-start(f32[128,128]{1,0:T(8,128)} %copy-done.18) | copy-start | bytes 196612
  368.0 23.4 %copy-start.11 = (f32[128,2,128]{2,1,0:T(2,128)S(1)}, f32[128,2,128]{2,1,0:T(2,128)}, u32[]{:S(2)}) copy-start(f32[128,2,128]{2,1,0:T(2,128)} %copy-done.10) | copy-start | bytes 393220
  368.0 50.7 %copy-start.1 = (bf16[1,128,1536]{2,1,0:T(8,128)(2,1)S(1)}, bf16[1,128,1536]{2,1,0:T(8,128)(2,1)}, u32[]{:S(2)}) copy-start(bf16[1,128,1536]{2,1,0:T(8,128)(2,1)} %param.11) | copy-start | bytes 1179652
  368.0 50.7 %copy-start.22 = (f32[128]{0:T(128)S(1)}, f32[128]{0:T(128)}, u32[]{:S(2)}) copy-start(f32[128]{0:T(128)} %copy-done.21) | copy-start | bytes 1540
  371.6 176.8 %reduce-scatter.22.cloned.1.call-start = ((), (), s32[]{:S(2)}) async-start(), calls=%async_computation.13 | async-start | bytes 12386304 | tf_op jit(solution)/shard_map/reduce_scatter | solution.py:317
  417.7 2.9 slice-start
  418.7 2.2 slice-start.1
  435.1 141.6 %reduce-scatter.28.cloned.1.call-start = ((), (), s32[]{:S(2)}) async-start(), calls=%async_computation.17 | async-start | bytes 442368
  435.3 8.3 %copy-start.26 = (bf16[1024,1536]{1,0:T(8,128)(2,1)S(1)}, bf16[1024,1536]{1,0:T(8,128)(2,1)}, u32[]{:S(2)}) copy-start(bf16[1024,1536]{1,0:T(8,128)(2,1)} %all-gather.9.cloned.1.call-done) | copy-start | bytes 9437188
  435.3 8.3 %copy-start.31 = (bf16[1024,1120]{0,1:T(8,128)(2,1)S(1)}, bf16[1024,1120]{0,1:T(8,128)(2,1)}, u32[]{:S(2)}) copy-start(bf16[1024,1120]{0,1:T(8,128)(2,1)} %copy-done.30) | copy-start | bytes 6881284
  443.6 5.3 copy-start.33
  443.7 10.5 %slice-start.2 = ((s8[11010048]{0:T(1024)(128)(4,1)}), s8[4194304]{0:T(1024)(128)(4,1)S(1)}, s32[]{:S(2)}) async-start(s8[11010048]{0:T(1024)(128)(4,1)} %bitcast.172), calls=%async_computation.21 | async-start | bytes 8388608
  443.7 10.5 %slice-start.3 = ((s8[11010048]{0:T(1024)(128)(4,1)}), s8[4194304]{0:T(1024)(128)(4,1)S(1)}, s32[]{:S(2)}) async-start(s8[11010048]{0:T(1024)(128)(4,1)} %bitcast.172), calls=%async_computation.22 | async-start | bytes 8388608
  448.9 5.2 copy-start.20
  448.9 5.2 slice-start.4
  456.4 229.8 %reduce-scatter.30.cloned.1.call-start = ((), (), s32[]{:S(2)}) async-start(), calls=%async_computation.18 | async-start | bytes 12902400
  466.0 82.5 %copy-start.29 = (u32[32]{0:T(128)S(1)}, u32[32]{0:T(128)}, u32[]{:S(2)}) copy-start(u32[32]{0:T(128)} %constant.86) | copy-start | bytes 388
  466.0 83.1 %copy-start.28 = (u32[32]{0:T(128)S(1)}, u32[32]{0:T(128)}, u32[]{:S(2)}) copy-start(u32[32]{0:T(128)} %constant.90) | copy-start | bytes 388
  466.1 252.9 %reduce-scatter.24.cloned.1.call-start = ((), (), s32[]{:S(2)}) async-start(), calls=%async_computation.14 | async-start | bytes 1720320 | tf_op jit(solution)/shard_map/reduce_scatter | solution.py:328
  (2 other events, 1.4 us)
Sparse Core Ops, SparseCore 0:
  10.5 103.6 all-gather.6
  152.9 40.0 all-gather.8
  194.7 37.1 all-gather.10
  260.7 37.9 reduce-scatter.17
  300.8 39.4 reduce-scatter.15
  365.3 24.7 reduce-scatter.19
  393.6 24.0 reduce-scatter.25
  435.2 113.1 reduce-scatter.21
  551.3 25.3 reduce-scatter.27
  580.0 106.2 reduce-scatter.29
  689.2 29.7 reduce-scatter.23

commit v2 on v0

v2 whole, which is shorter than its diff:
```python
import jax
import jax.numpy as jnp
from jax import lax
from jax.sharding import PartitionSpec as P

HEADS = 12
KV_HEADS = 2
HEAD_DIM = 128


EPSILON = 1e-06
THETA = 10000.0
LOW = jnp.bfloat16
FULL = jnp.float32


def rope_tables(positions, width):
    half = width // 2
    frequency = THETA ** (-(jnp.arange(half, dtype=jnp.float32) * 2.0 / width))
    angle = positions.astype(jnp.float32)[:, None] * frequency[None, :]
    cosine = jnp.concatenate([jnp.cos(angle), jnp.cos(angle)], axis=1)
    sine = jnp.concatenate([jnp.sin(angle), jnp.sin(angle)], axis=1)
    return (cosine, sine)


def rotate(vectors, cosine, sine):
    half = vectors.shape[-1] // 2
    turned = jnp.concatenate([-vectors[..., half:], vectors[..., :half]], axis=-1)
    return vectors * cosine[:, None, :] + turned * sine[:, None, :]


def unrotate(gradient, cosine, sine):
    half = gradient.shape[-1] // 2
    moved = gradient * sine[:, None, :]
    return gradient * cosine[:, None, :] + jnp.concatenate(
        [moved[..., half:], -moved[..., :half]], axis=-1
    )


def segments(starts, positions):
    return jnp.sum((starts[None, :] <= positions[:, None]).astype(jnp.int32), axis=1) - 1


def inverse_rms(values):
    return lax.rsqrt(jnp.mean(values * values, axis=-1, keepdims=True) + EPSILON)


def norm_backward(inputs, scale, gain, back_normed):
    weighted = back_normed * gain
    back_inputs = scale * weighted - inputs * scale * scale * scale * jnp.mean(
        inputs * weighted, axis=-1, keepdims=True
    )
    return (back_inputs, jnp.sum(back_normed * inputs * scale, axis=0))


def matmul(equation, left, right):
    return jnp.einsum(equation, left, right, preferred_element_type=FULL)


class Ring:
    def __init__(self, size):
        self.size = size
        self.chips = size // 2

    def shift(self, block, chips):
        moves = [(i, (i + 2 * chips) % self.size) for i in range(self.size)]
        return lax.ppermute(block, "fsdp", moves)

    def swap(self, block):
        return lax.ppermute(block, "fsdp", [(i, i ^ 1) for i in range(self.size)])

    def gather(self, block):
        own = [block] + [self.shift(block, d) for d in range(1, self.chips)]
        return own + [self.swap(b) for b in own]

    def reduce(self, parts):
        other = self.swap(parts[self.chips :])
        summed = [
            (parts[d].astype(FULL) + other[d].astype(FULL)).astype(LOW) for d in range(self.chips)
        ]
        return [summed[0]] + [self.shift(summed[d], -d) for d in range(1, self.chips)]

    def exchange(self, pieces):
        index = lax.axis_index("fsdp")
        chip, core = index // 2, index % 2
        by_chip = pieces.reshape((self.chips, 2) + pieces.shape[1:])
        mine = lax.dynamic_index_in_dim(by_chip, core, 1, keepdims=False)
        theirs = self.swap(lax.dynamic_index_in_dim(by_chip, 1 - core, 1, keepdims=False))
        pair = jnp.stack([mine, theirs], axis=1)
        got = []
        for d in range(self.chips):
            target = lax.rem(chip + d, self.chips)
            block = lax.dynamic_index_in_dim(pair, target, 0, keepdims=False)
            got.append(self.shift(block, d) if d else block)
        return [g[0] for g in got] + [g[1] for g in got]


def ctx_scatter(pieces):
    count = pieces.shape[0]
    me = lax.axis_index("ctx")
    terms = [lax.dynamic_index_in_dim(pieces, me, 0, keepdims=False)]
    for d in range(1, count):
        moves = [(i, i ^ d) for i in range(count)]
        terms.append(
            lax.ppermute(
                lax.dynamic_index_in_dim(pieces, me ^ d, 0, keepdims=False), "ctx", moves
            )
        )
    return terms


def total_of(terms):
    result = terms[0].astype(FULL)
    for term in terms[1:]:
        result = result + term.astype(FULL)
    return result


def make(ring, contexts):
    def per_device(
        tokens,
        document_starts,
        attention_weights,
        projection_bias,
        norm_gains,
        hidden_weights,
        cotangent,
    ):
        rows = tokens.shape[1]
        width = tokens.shape[2]
        group = HEADS // KV_HEADS
        query_width = HEADS * HEAD_DIM
        key_width = KV_HEADS * HEAD_DIM
        projection_width = query_width + 2 * key_width
        scale = HEAD_DIM ** (-0.5)
        size = ring.size
        me = lax.axis_index("ctx")
        own_rows = attention_weights.shape[0]
        quarter = own_rows // contexts

        starts = document_starts[0]
        positions = me * rows + jnp.arange(rows, dtype=jnp.int32)
        query_segment = segments(starts, positions)
        cosine, sine = rope_tables(positions, HEAD_DIM)

        weight_piece = lax.dynamic_slice_in_dim(attention_weights, me * quarter, quarter, 0)
        block_weights = lax.all_gather(
            weight_piece.astype(LOW), ("fsdp", "ctx"), axis=0, tiled=True
        )
        gain_width = norm_gains.shape[1]
        packed = jnp.concatenate([projection_bias, norm_gains.reshape(-1)]).astype(LOW)
        packed_all = lax.all_gather(packed, "fsdp", axis=0)
        bias_width = projection_bias.shape[0]
        bias_all = packed_all[:, :bias_width].reshape(-1).astype(FULL)
        gain_one = packed_all[:, bias_width : bias_width + gain_width].reshape(-1).astype(FULL)
        gain_two = packed_all[:, bias_width + gain_width :].reshape(-1).astype(FULL)

        upstream = cotangent[0]
        upstream_all = jnp.concatenate(ring.gather(upstream), axis=0)
        tokens_all = jnp.concatenate(ring.gather(tokens[0]), axis=0)
        hidden_low = hidden_weights.astype(LOW)
        gate_rows = hidden_low[:, :width]
        up_rows = hidden_low[:, width : 2 * width]
        down_rows = hidden_low[:, 2 * width :]
        back_hidden = matmul("td,fd->tf", upstream_all, down_rows)
        inputs_all = tokens_all.astype(FULL)
        normed_one_all = (inputs_all * inverse_rms(inputs_all) * gain_one).astype(LOW)

        w_project = block_weights[:projection_width]
        w_output = block_weights[projection_width:]
        inputs = tokens[0].astype(FULL)
        scale_one = inverse_rms(inputs)
        normed_one = (inputs * scale_one * gain_one).astype(LOW)
        projected = matmul("td,rd->tr", normed_one, w_project) + bias_all
        queries = rotate(
            projected[:, :query_width].reshape(rows, HEADS, HEAD_DIM), cosine, sine
        ).astype(LOW)
        queries = queries.reshape(rows, KV_HEADS, group, HEAD_DIM)
        keys = rotate(
            projected[:, query_width : query_width + key_width].reshape(rows, KV_HEADS, HEAD_DIM),
            cosine,
            sine,
        )
        keys = keys.astype(LOW).reshape(rows, key_width)
        values = projected[:, query_width + key_width :].astype(LOW)
        both_all = lax.all_gather(
            jnp.concatenate([keys, values], axis=1), "ctx", axis=0, tiled=True
        )
        count = both_all.shape[0]
        keys_all = both_all[:, :key_width].reshape(count, KV_HEADS, HEAD_DIM)
        values_all = both_all[:, key_width:].reshape(count, KV_HEADS, HEAD_DIM)
        key_positions = jnp.arange(count, dtype=jnp.int32)
        mask = (query_segment[:, None] == segments(starts, key_positions)[None, :]) & (
            key_positions[None, :] <= positions[:, None]
        )
        scores = matmul("tkgd,skd->kgts", queries, keys_all) * scale
        scores = jnp.where(mask, scores, -jnp.inf)
        top = jnp.max(scores, axis=-1, keepdims=True)
        raised = jnp.exp(scores - top)
        probability = raised / jnp.sum(raised, axis=-1, keepdims=True)
        probability_low = probability.astype(LOW)
        attention_out = matmul("kgts,skd->kgtd", probability_low, values_all)
        mixed_low = attention_out.transpose(2, 0, 1, 3).reshape(rows, query_width).astype(LOW)
        residual = inputs + matmul("tf,fd->td", mixed_low, w_output)
        scale_two = inverse_rms(residual)
        normed_two = (residual * scale_two * gain_two).astype(LOW)

        normed_all = jnp.concatenate(ring.gather(normed_two), axis=0)
        gate_value = matmul("td,fd->tf", normed_all, gate_rows)
        up_value = matmul("td,fd->tf", normed_all, up_rows)
        sigmoid_gate = jax.nn.sigmoid(gate_value)
        silu_gate = gate_value * sigmoid_gate
        hidden = (silu_gate * up_value).astype(LOW)
        back_up = (back_hidden * silu_gate).astype(LOW)
        back_gate = (
            back_hidden * up_value * sigmoid_gate * (1.0 + gate_value * (1.0 - sigmoid_gate))
        ).astype(LOW)
        back_normed_part = matmul("tf,fd->td", back_gate, gate_rows) + matmul(
            "tf,fd->td", back_up, up_rows
        )
        back_normed_two = total_of(
            ring.reduce(back_normed_part.astype(LOW).reshape(size, rows, width))
        )
        lifted_part = matmul("tf,fd->td", hidden, down_rows)
        lifted = total_of(ring.reduce(lifted_part.astype(LOW).reshape(size, rows, width)))
        output = (residual + lifted).astype(LOW)
        hidden_term = jnp.concatenate(
            [
                matmul("tf,td->fd", back_gate, normed_all),
                matmul("tf,td->fd", back_up, normed_all),
                matmul("tf,td->fd", hidden, upstream_all),
            ],
            axis=1,
        ).astype(LOW)
        hidden_shard = lax.psum_scatter(
            hidden_term, "ctx", scatter_dimension=0, tiled=True
        ).astype(FULL)

        back_residual_part, back_gain_two = norm_backward(
            residual, scale_two, gain_two, back_normed_two
        )
        back_residual = upstream.astype(FULL) + back_residual_part
        back_branch = back_residual.astype(LOW)
        back_branch_all = jnp.concatenate(ring.gather(back_branch), axis=0)
        back_mixed = matmul("td,fd->tf", back_branch, w_output).astype(LOW)
        back_mixed = back_mixed.reshape(rows, KV_HEADS, group, HEAD_DIM)
        delta = jnp.sum(
            back_mixed.transpose(1, 2, 0, 3).astype(FULL) * attention_out, axis=-1, keepdims=True
        )
        back_probability = matmul("tkgd,skd->kgts", back_mixed, values_all)
        back_scores = (probability * (back_probability - delta)).astype(LOW)
        back_query = matmul("kgts,skd->kgtd", back_scores, keys_all) * scale
        back_keys = matmul("kgts,tkgd->skd", back_scores, queries) * scale
        back_values = matmul("kgts,tkgd->skd", probability_low, back_mixed)
        back_both = jnp.concatenate(
            [back_keys.reshape(count, key_width), back_values.reshape(count, key_width)], axis=1
        ).astype(LOW)
        back_both_own = total_of(ctx_scatter(back_both.reshape(contexts, rows, 2 * key_width)))
        back_query_heads = back_query.transpose(2, 0, 1, 3).reshape(rows, HEADS, HEAD_DIM)
        back_query_pre = unrotate(back_query_heads, cosine, sine).reshape(rows, query_width)
        back_key_pre = unrotate(
            back_both_own[:, :key_width].reshape(rows, KV_HEADS, HEAD_DIM), cosine, sine
        ).reshape(rows, key_width)
        back_projected = jnp.concatenate(
            [back_query_pre, back_key_pre, back_both_own[:, key_width:]], axis=1
        ).astype(LOW)
        back_bias = jnp.sum(back_projected.astype(FULL), axis=0)
        back_normed_one = matmul("tr,rd->td", back_projected, w_project)
        back_inputs_part, back_gain_one = norm_backward(
            inputs, scale_one, gain_one, back_normed_one
        )
        back_inputs = back_residual + back_inputs_part

        def by_owner(block):
            return block.reshape(rows, size, own_rows).transpose(1, 0, 2)

        mixed_pieces = by_owner(
            jnp.concatenate([jnp.zeros((rows, projection_width), LOW), mixed_low], axis=1)
        )
        mixed_columns = jnp.concatenate(ring.exchange(mixed_pieces), axis=0)
        projected_pieces = by_owner(
            jnp.concatenate([back_projected, jnp.zeros((rows, query_width), LOW)], axis=1)
        )
        small = jnp.concatenate(
            [
                back_bias.reshape(size, 1, bias_width),
                jnp.zeros((size, 1, own_rows - bias_width), FULL),
            ],
            axis=2,
        )
        gains_small = jnp.concatenate(
            [
                jnp.stack([back_gain_one, back_gain_two], axis=0)
                .reshape(2, size, gain_width)
                .transpose(1, 0, 2),
                jnp.zeros((size, 2, own_rows - gain_width), FULL),
            ],
            axis=2,
        )
        small = jnp.concatenate([small, gains_small, jnp.zeros((size, 13, own_rows), FULL)], axis=1)
        projected_got = ring.exchange(
            jnp.concatenate([projected_pieces, small.astype(LOW)], axis=1)
        )
        projected_columns = jnp.concatenate([g[:rows] for g in projected_got], axis=0)
        small_sum = total_of([g[rows : rows + 3] for g in projected_got])

        attention_term = (
            matmul("tr,td->rd", projected_columns, normed_one_all)
            + matmul("tr,td->rd", mixed_columns, back_branch_all)
        ).astype(LOW)
        own_bias = bias_width // contexts
        own_gain = gain_width // contexts
        tail = jnp.concatenate(
            [
                small_sum[0, :bias_width].reshape(contexts, 1, own_bias),
                small_sum[1, :gain_width].reshape(contexts, 1, own_gain),
                small_sum[2, :gain_width].reshape(contexts, 1, own_gain),
                jnp.zeros((contexts, 1, width - own_bias - 2 * own_gain), FULL),
            ],
            axis=2,
        )
        tail = jnp.concatenate([tail, jnp.zeros((contexts, 15, width), FULL)], axis=1).astype(LOW)
        shards = total_of(
            ctx_scatter(
                jnp.concatenate([attention_term.reshape(contexts, quarter, width), tail], axis=1)
            )
        )
        attention_shard = shards[:quarter]
        bias_shard = shards[quarter, :own_bias]
        gain_shard = shards[quarter, own_bias : own_bias + 2 * own_gain].reshape(2, own_gain)
        return (
            output[None],
            back_inputs[None],
            attention_shard,
            bias_shard,
            gain_shard,
            hidden_shard,
        )

    return per_device


def solution(mesh):
    placed = (
        P("fsdp", "ctx", None),
        P("fsdp", None),
        P("fsdp", None),
        P("fsdp"),
        P(None, "fsdp"),
        P("fsdp", None),
        P("fsdp", "ctx", None),
    )
    return jax.shard_map(
        make(Ring(mesh.shape["fsdp"]), mesh.shape["ctx"]),
        mesh=mesh,
        in_specs=placed,
        out_specs=(
            P("fsdp", "ctx", None),
            P("fsdp", "ctx", None),
            P(("fsdp", "ctx"), None),
            P(("fsdp", "ctx")),
            P(None, ("fsdp", "ctx")),
            P(("fsdp", "ctx"), None),
        ),
        check_vma=False,
    )
```

time: 2260 us -> 527 us (0.23)
  waiting for transfers between devices: 1770 us -> 163 us
  local copies, waits for them, and re-layouts: 146 us -> 60.2 us
  starting transfers between devices: 0.83 us -> 69.9 us
  other arithmetic: 114 us -> 49.2 us
  matrix products: 156 us -> 91.7 us
    unnamed x13 -> x3, waiting for transfers between devices: 1010 us -> 0.03 us
    all_gather x2 -> x1, waiting for transfers between devices: 726 us -> 0.01 us  [per_device(): lax.all_gather(weight_piece.astype(LOW), ('fsdp', 'ctx'), axis=0, tiled=T...]
    ppermute x0 -> x50, waiting for transfers between devices: none -> 163 us  [the longest x24 144 us: shift(): return lax.ppermute(block, 'fsdp', moves)]
    unnamed x94 -> x149, local copies, waits for them, and re-layouts: 132 us -> 37.4 us
    ppermute x0 -> x50, starting transfers between devices: none -> 69.8 us  [the longest x20 32.5 us: swap(): return lax.ppermute(block, 'fsdp', [(i, i ^ 1) for i in range(self.size)])]
    dot_general x21 -> x20, matrix products: 154 us -> 89 us  [matmul(): return jnp.einsum(equation, left, right, preferred_element_type=FULL)]
    concatenate x2 -> x4, other arithmetic: 71.3 us -> 6.35 us  [the longest x1 4.43 us: per_device(): jnp.concatenate([matmul('tf,td->fd', back_gate, normed_all), matmul('tf,t...]
    all_gather x4 -> x2, blocking collectives: 34.6 us -> 68.6 us  [the longest x1 59.4 us: per_device(): packed_all = lax.all_gather(packed, 'fsdp', axis=0)]
  transfers between devices with their start and end apart: 9 -> 52, of which waited for: 7 -> 18; matrix products, arithmetic and copies ran while one was open for 13% -> 36% of each run, Pallas kernels for 0% -> 0%
where the time goes in v2:
time: 527 us; the launch traced here: 519 us
  waiting for transfers between devices  163 us (31%)
  matrix products  91.7 us (17%)
  starting transfers between devices  69.9 us (13%)
  blocking collectives  68.6 us (13%)
  local copies, waits for them, and re-layouts  60.2 us (11%)
  other arithmetic  49.2 us (9%)
  between operations  15.9 us (3%)
    ppermute x24, waiting for transfers between devices, shift(): return lax.ppermute(block, 'fsdp', moves)  144 us
    dot_general x20, matrix products, matmul(): return jnp.einsum(equation, left, right, preferred_element_type=FULL)  89 us
    all_gather x1, blocking collectives, per_device(): packed_all = lax.all_gather(packed, 'fsdp', axis=0)  59.4 us
    unnamed x149, local copies, waits for them, and re-layouts  37.4 us
    ppermute x20, starting transfers between devices, swap(): return lax.ppermute(block, 'fsdp', [(i, i ^ 1) for i in range(self.size)])  32.5 us
    ppermute x24, starting transfers between devices, shift(): return lax.ppermute(block, 'fsdp', moves)  32 us
    ppermute x6, waiting for transfers between devices, ctx_scatter(): lax.ppermute(lax.dynamic_index_in_dim(pieces, me ^ d, 0, keepdims=False),...  16.9 us
    convert_element_type x1, other arithmetic, per_device(): hidden_low = hidden_weights.astype(LOW)  12.7 us
  transfers between devices with their start and end apart: 52, of which 18 were waited for; matrix products, arithmetic and copies ran while one was open for 36% of the time, Pallas kernels for 0%

profile of v2, /device:TPU:17, one launch (start us, length us, event | category | flops | bytes accessed | tf_op | source)
XLA Modules:
  0.0 518.8 jit_solution(14175823556180708283)
XLA Ops:
  15.6 59.4 %all-gather = bf16[8,1,640]{2,1,0:T(2,128)(2,1)S(1)} all-gather(bf16[1,1,640]{2,1,0:T(2,128)(2,1)S(1)} %maximum_bitcast_fusion.1), channel_id=1, replica_groups=mesh['ctx'=4,'fsdp'=8] {'fsdp'}, dimensions={0}, use_global_device_ids=true | all-gather | bytes 11520 | tf_op jit(solution)/shard_map/all_gather | solution.py:152
  81.0 12.7 %convert_element_type.361 = bf16[1120,4608]{1,0:T(8,128)(2,1)} convert(f32[1120,4608]{1,0:T(8,128)} %param.12) | non-fusion elementwise | flops 5160960 | bytes 30965760 | tf_op jit(solution)/shard_map/convert_element_type | solution.py:161
  103.9 24.7 %collective-permute-done.30 = bf16[128,1536]{1,0:T(8,128)(2,1)} collective-permute-done((bf16[128,1536]{1,0:T(8,128)(2,1)S(1)}, bf16[128,1536]{1,0:T(8,128)(2,1)}, u32[]{:S(2)}, u32[]{:S(2)}) %collective-permute-start.30) | collective-permute-done | bytes 393248 | tf_op jit(solution)/shard_map/ppermute | solution.py:67
  131.2 8.1 %collective-permute-done.31 = bf16[128,1536]{1,0:T(8,128)(2,1)} collective-permute-done((bf16[128,1536]{1,0:T(8,128)(2,1)S(1)}, bf16[128,1536]{1,0:T(8,128)(2,1)}, u32[]{:S(2)}, u32[]{:S(2)}) %collective-permute-start.31) | collective-permute-done | bytes 393248 | tf_op jit(solution)/shard_map/ppermute | solution.py:67
  143.6 4.9 fusion.39
  152.0 9.2 %all_gather.12 = bf16[512,512]{1,0:T(8,128)(2,1)S(1)} all-gather(bf16[128,512]{1,0:T(8,128)(2,1)S(1)} %pad_maximum_fusion.3), channel_id=1, replica_groups=mesh['ctx'=4,'fsdp'=8] {'ctx'}, dimensions={0}, use_global_device_ids=true | all-gather | bytes 655360 | tf_op jit(solution)/shard_map/all_gather | solution.py:186
  163.6 2.7 fusion.150
  166.3 2.4 fusion.54
  170.0 3.4 multiply_reduce_fusion.2
  176.5 2.0 collective-permute-start.1
  179.6 4.7 collective-permute-done
  185.6 15.3 %collective-permute-done.1 = bf16[128,1536]{1,0:T(8,128)(2,1)S(1)} collective-permute-done((bf16[128,1536]{1,0:T(8,128)(2,1)S(1)}, bf16[128,1536]{1,0:T(8,128)(2,1)S(1)}, u32[]{:S(2)}, u32[]{:S(2)}) %collective-permute-start.1) | collective-permute-done | bytes 393248 | tf_op jit(solution)/shard_map/ppermute | solution.py:67
  200.9 4.2 collective-permute-start.3
  205.2 7.6 %collective-permute-start.4 = (bf16[128,1536]{1,0:T(8,128)(2,1)S(1)}, bf16[128,1536]{1,0:T(8,128)(2,1)S(1)}, u32[]{:S(2)}, u32[]{:S(2)}) collective-permute-start(bf16[128,1536]{1,0:T(8,128)(2,1)S(1)} %collective-permute-done), channel_id=1, source_target_pairs={{0,1},{1,0},{2,3},{3,2},{4,5},{5,4},{6,7},{7,6},{8,9},{9,8},{10,11... | collective-permute-start | bytes 1179656 | tf_op jit(solution)/shard_map/ppermute | solution.py:70
  215.9 5.4 %fusion.31 = f32[1024,1120]{0,1:T(8,128)} fusion(bf16[1024,1536]{1,0:T(8,128)(2,1)S(1)} %constant_dynamic-update-slice_fusion, bf16[1120,4608]{1,0:T(8,128)(2,1)S(1)} %bitcast.354), kind=kOutput, calls=%fused_computation.48 | convolution fusion | flops 3523215360 | bytes 11173888 | tf_op jit(solution)/shard_map/td,fd->tf/dot_general | solution.py:57
  221.3 5.3 %fusion.27 = f32[1024,1120]{0,1:T(8,128)} fusion(bf16[1024,1536]{1,0:T(8,128)(2,1)S(1)} %constant_dynamic-update-slice_fusion, bf16[1120,4608]{1,0:T(8,128)(2,1)S(1)} %bitcast.354), kind=kOutput, calls=%fused_computation.44 | convolution fusion | flops 3523215360 | bytes 11173888 | tf_op jit(solution)/shard_map/td,fd->tf/dot_general | solution.py:57
  226.6 9.6 %multiply_convert_fusion = (bf16[1024,1120]{0,1:T(8,128)(2,1)}, bf16[1024,1120]{0,1:T(8,128)(2,1)}, bf16[1024,1120]{0,1:T(8,128)(2,1)}) fusion(f32[1024,1120]{0,1:T(8,128)} %fusion.31, f32[1024,1120]{0,1:T(8,128)} %fusion.27, bf16[1024,1536]{1,0:T(8,128)(2,1)S(1)} %constant_dynamic-update-slice_fusion.8, bf16[1120,4608]{1,0:T(8,128)(2,1)S(1)} %bitcast.354), kind=kOutput, calls=%fused_computation.15 | convolution fusion | flops 3540418560 | bytes 22642688 | tf_op jit(solution)/shard_map/td,fd->tf/dot_general | solution.py:57
  236.2 5.7 %convolution_convert_fusion = bf16[1120,1536]{1,0:T(8,128)(2,1)S(1)} fusion(bf16[1024,1120]{0,1:T(8,128)(2,1)} %get-tuple-element.21, bf16[1024,1536]{1,0:T(8,128)(2,1)S(1)} %constant_dynamic-update-slice_fusion.8), kind=kOutput, calls=%fused_computation.4 | convolution fusion | flops 3524935680 | bytes 8880128 | tf_op jit(solution)/shard_map/tf,td->fd/dot_general | solution.py:57
  242.0 4.0 convolution_convert_fusion.1
  245.9 4.0 convolution_convert_fusion.2
  249.9 4.4 pad_maximum_fusion
  260.3 2.1 copy-done.2
  265.5 15.0 %collective-permute-done.37 = bf16[2,128,448]{1,2,0:T(8,128)(2,1)S(1)} collective-permute-done((bf16[2,128,448]{1,2,0:T(8,128)(2,1)S(1)}, bf16[2,128,448]{1,2,0:T(8,128)(2,1)S(1)}, u32[]{:S(2)}, u32[]{:S(2)}) %collective-permute-start.37) | collective-permute-done | bytes 229408 | tf_op jit(solution)/shard_map/ppermute | solution.py:67
  280.7 6.9 %fusion.29 = f32[1024,1536]{1,0:T(8,128)S(1)} fusion(bf16[1024,1120]{0,1:T(8,128)(2,1)S(1)} %copy-done.45, bf16[1120,4608]{1,0:T(8,128)(2,1)} %convert_element_type.361), kind=kOutput, calls=%fused_computation.46 | convolution fusion | flops 3523215360 | bytes 12025856 | tf_op jit(solution)/shard_map/tf,fd->td/dot_general | solution.py:57
  287.6 4.9 add_convert_fusion
  294.6 4.7 convolution_convert_fusion.3
  301.5 5.5 %collective-permute-start.21 = (bf16[128,1536]{1,0:T(8,128)(2,1)S(1)}, bf16[128,1536]{1,0:T(8,128)(2,1)S(1)}, u32[]{:S(2)}, u32[]{:S(2)}) collective-permute-start(bf16[128,1536]{1,0:T(8,128)(2,1)S(1)} %get-tuple-element.23), channel_id=1, source_target_pairs={{0,2},{1,3},{2,4},{3,5},{4,6},{5,7},{6,0},{7,1},{8,10},{9,11},{10,... | collective-permute-start | bytes 1179656 | tf_op jit(solution)/shard_map/ppermute | solution.py:67
  312.4 4.4 collective-permute-done.21
  316.8 15.7 %collective-permute-done.20 = bf16[128,1536]{1,0:T(8,128)(2,1)S(1)} collective-permute-done((bf16[128,1536]{1,0:T(8,128)(2,1)S(1)}, bf16[128,1536]{1,0:T(8,128)(2,1)S(1)}, u32[]{:S(2)}, u32[]{:S(2)}) %collective-permute-start.20) | collective-permute-done | bytes 393248 | tf_op jit(solution)/shard_map/ppermute | solution.py:67
  332.5 25.3 %collective-permute-done.19 = bf16[128,1536]{1,0:T(8,128)(2,1)S(1)} collective-permute-done((bf16[128,1536]{1,0:T(8,128)(2,1)S(1)}, bf16[128,1536]{1,0:T(8,128)(2,1)S(1)}, u32[]{:S(2)}, u32[]{:S(2)}) %collective-permute-start.19) | collective-permute-done | bytes 393248 | tf_op jit(solution)/shard_map/ppermute | solution.py:67
  360.7 4.7 fusion.42
  368.7 4.0 fusion.16
  372.6 2.8 fusion.61
  378.9 2.3 fusion.62
  384.3 2.3 collective-permute-start.23
  391.3 2.4 collective-permute-done.23
  400.0 5.4 %fusion.74 = (bf16[1536]{0:T(1024)(128)(2,1)S(1)}, f32[128]{0:T(128)}, f32[128,1536]{1,0:T(8,128)}) fusion(f32[128]{0:T(128)} %copy-done.39, bf16[1,128,1536]{2,1,0:T(8,128)(2,1)S(1)} %copy-done.5, f32[1536]{0:T(1024)S(1)} %reshape.298, bf16[128,2048]{0,1:T(8,128)(2,1)S(1)} %get-tuple-element.15, bf16[3584,1536]{1,0:T(8,128)(2,1)} %all-gather.3.cloned.1.call-done), kind=kOutput, calls=%fused_computation.107 | convolution fusion | flops 806680960 | bytes 8005632 | tf_op jit(solution)/shard_map/tr,rd->td/dot_general | solution.py:57
  411.1 11.1 %collective-permute-start.43 = (bf16[128,1536]{1,0:T(8,128)(2,1)S(1)}, bf16[128,1536]{1,0:T(8,128)(2,1)S(1)}, u32[]{:S(2)}, u32[]{:S(2)}) collective-permute-start(bf16[128,1536]{1,0:T(8,128)(2,1)S(1)} %copy-done.24), channel_id=1, source_target_pairs={{0,1},{1,0},{2,3},{3,2},{4,5},{5,4},{6,7},{7,6},{8,9},{9,8},{10,11... | collective-permute-start | bytes 1179656 | tf_op jit(solution)/shard_map/ppermute | solution.py:70
  427.5 4.6 collective-permute-start.28
  432.2 4.1 collective-permute-start.27
  436.4 3.1 fusion.152
  441.3 15.7 %collective-permute-done.27 = bf16[2,144,448]{2,1,0:T(8,128)(2,1)S(1)} collective-permute-done((bf16[2,144,448]{2,1,0:T(8,128)(2,1)S(1)}, bf16[2,144,448]{2,1,0:T(8,128)(2,1)S(1)}, u32[]{:S(2)}, u32[]{:S(2)}) %collective-permute-start.27) | collective-permute-done | bytes 258080 | tf_op jit(solution)/shard_map/ppermute | solution.py:67
  457.1 13.3 %collective-permute-done.26 = bf16[2,144,448]{2,1,0:T(8,128)(2,1)S(1)} collective-permute-done((bf16[2,144,448]{2,1,0:T(8,128)(2,1)S(1)}, bf16[2,144,448]{2,1,0:T(8,128)(2,1)S(1)}, u32[]{:S(2)}, u32[]{:S(2)}) %collective-permute-start.26) | collective-permute-done | bytes 258080 | tf_op jit(solution)/shard_map/ppermute | solution.py:67
  478.7 4.8 fusion.33
  486.6 3.1 fusion.70
  489.7 4.9 collective-permute-done.49
  494.6 9.6 %collective-permute-done.48 = bf16[128,1536]{1,0:T(8,128)(2,1)S(1)} collective-permute-done((bf16[128,1536]{1,0:T(8,128)(2,1)S(1)}, bf16[128,1536]{1,0:T(8,128)(2,1)S(1)}, u32[]{:S(2)}, u32[]{:S(2)}) %collective-permute-start.48) | collective-permute-done | bytes 393248 | tf_op jit(solution)/shard_map/ppermute | solution.py:105
  506.5 4.9 convert_element_type.444
  (348 shorter events, 115.5 us)
Async XLA Ops:
  7.2 136.4 %all-gather.3.cloned.1.call-start = ((), (), s32[]{:S(2)}) async-start(), calls=%async_computation.1 | async-start | bytes 11354112 | tf_op jit(solution)/shard_map/all_gather | solution.py:147
  9.7 496.8 %reduce-scatter.4.cloned.1.call-start = ((), (), s32[]{:S(2)}) async-start(), calls=%async_computation.2 | async-start | bytes 12902400
  9.8 84.7 %collective-permute-start.11 = (bf16[128,1536]{1,0:T(8,128)(2,1)}, bf16[128,1536]{1,0:T(8,128)(2,1)S(1)}, u32[]{:S(2)}, u32[]{:S(2)}) collective-permute-start(bf16[128,1536]{1,0:T(8,128)(2,1)} %bitcast.363), channel_id=1, source_target_pairs={{0,2},{1,3},{2,4},{3,5},{4,6},{5,7},{6,0},{7,1},{8,10},{9,11},{10,... | collective-permute-start | bytes 1179656 | tf_op jit(solution)/shard_map/ppermute | solution.py:67
  11.1 85.7 %collective-permute-start.12 = (bf16[128,1536]{1,0:T(8,128)(2,1)}, bf16[128,1536]{1,0:T(8,128)(2,1)}, u32[]{:S(2)}, u32[]{:S(2)}) collective-permute-start(bf16[128,1536]{1,0:T(8,128)(2,1)} %bitcast.364), channel_id=1, source_target_pairs={{0,4},{1,5},{2,6},{3,7},{4,0},{5,1},{6,2},{7,3},{8,12},{9,13},{10,... | collective-permute-start | bytes 1179656 | tf_op jit(solution)/shard_map/ppermute | solution.py:67
  11.2 87.4 %collective-permute-start.13 = (bf16[128,1536]{1,0:T(8,128)(2,1)}, bf16[128,1536]{1,0:T(8,128)(2,1)}, u32[]{:S(2)}, u32[]{:S(2)}) collective-permute-start(bf16[128,1536]{1,0:T(8,128)(2,1)} %bitcast.365), channel_id=1, source_target_pairs={{0,6},{1,7},{2,0},{3,1},{4,2},{5,3},{6,4},{7,5},{8,14},{9,15},{10,... | collective-permute-start | bytes 1179656 | tf_op jit(solution)/shard_map/ppermute | solution.py:67
  12.4 88.4 %collective-permute-start.14 = (bf16[128,1536]{1,0:T(8,128)(2,1)}, bf16[128,1536]{1,0:T(8,128)(2,1)S(1)}, u32[]{:S(2)}, u32[]{:S(2)}) collective-permute-start(bf16[128,1536]{1,0:T(8,128)(2,1)} %bitcast.366), channel_id=1, source_target_pairs={{0,1},{1,0},{2,3},{3,2},{4,5},{5,4},{6,7},{7,6},{8,9},{9,8},{10,11... | collective-permute-start | bytes 1179656 | tf_op jit(solution)/shard_map/ppermute | solution.py:70
  13.6 88.0 %collective-permute-start.29 = (bf16[128,1536]{1,0:T(8,128)(2,1)}, bf16[128,1536]{1,0:T(8,128)(2,1)}, u32[]{:S(2)}, u32[]{:S(2)}) collective-permute-start(bf16[128,1536]{1,0:T(8,128)(2,1)} %bitcast.367), channel_id=1, source_target_pairs={{0,2},{1,3},{2,4},{3,5},{4,6},{5,7},{6,0},{7,1},{8,10},{9,11},{10,... | collective-permute-start | bytes 1179656 | tf_op jit(solution)/shard_map/ppermute | solution.py:67
  94.5 34.1 %collective-permute-start.30 = (bf16[128,1536]{1,0:T(8,128)(2,1)S(1)}, bf16[128,1536]{1,0:T(8,128)(2,1)}, u32[]{:S(2)}, u32[]{:S(2)}) collective-permute-start(bf16[128,1536]{1,0:T(8,128)(2,1)S(1)} %bitcast.368), channel_id=1, source_target_pairs={{0,4},{1,5},{2,6},{3,7},{4,0},{5,1},{6,2},{7,3},{8,12},{9,13},{10,... | collective-permute-start | bytes 1179656 | tf_op jit(solution)/shard_map/ppermute | solution.py:67
  96.8 42.5 %collective-permute-start.31 = (bf16[128,1536]{1,0:T(8,128)(2,1)S(1)}, bf16[128,1536]{1,0:T(8,128)(2,1)}, u32[]{:S(2)}, u32[]{:S(2)}) collective-permute-start(bf16[128,1536]{1,0:T(8,128)(2,1)S(1)} %bitcast.369), channel_id=1, source_target_pairs={{0,6},{1,7},{2,0},{3,1},{4,2},{5,3},{6,4},{7,5},{8,14},{9,15},{10,... | collective-permute-start | bytes 1179656 | tf_op jit(solution)/shard_map/ppermute | solution.py:67
  98.6 42.9 %collective-permute-start.32 = (bf16[128,1536]{1,0:T(8,128)(2,1)S(1)}, bf16[128,1536]{1,0:T(8,128)(2,1)S(1)}, u32[]{:S(2)}, u32[]{:S(2)}) collective-permute-start(bf16[128,1536]{1,0:T(8,128)(2,1)S(1)} %bitcast.370), channel_id=1, source_target_pairs={{0,1},{1,0},{2,3},{3,2},{4,5},{5,4},{6,7},{7,6},{8,9},{9,8},{10,11... | collective-permute-start | bytes 1179656 | tf_op jit(solution)/shard_map/ppermute | solution.py:70
  100.8 41.5 %collective-permute-start.15 = (bf16[128,1536]{1,0:T(8,128)(2,1)S(1)}, bf16[128,1536]{1,0:T(8,128)(2,1)S(1)}, u32[]{:S(2)}, u32[]{:S(2)}) collective-permute-start(bf16[128,1536]{1,0:T(8,128)(2,1)S(1)} %collective-permute-done.11), channel_id=1, source_target_pairs={{0,1},{1,0},{2,3},{3,2},{4,5},{5,4},{6,7},{7,6},{8,9},{9,8},{10,11... | collective-permute-start | bytes 1179656 | tf_op jit(solution)/shard_map/ppermute | solution.py:70
  101.6 72.0 %collective-permute-start.16 = (bf16[128,1536]{1,0:T(8,128)(2,1)}, bf16[128,1536]{1,0:T(8,128)(2,1)}, u32[]{:S(2)}, u32[]{:S(2)}) collective-permute-start(bf16[128,1536]{1,0:T(8,128)(2,1)} %collective-permute-done.12), channel_id=1, source_target_pairs={{0,1},{1,0},{2,3},{3,2},{4,5},{5,4},{6,7},{7,6},{8,9},{9,8},{10,11... | collective-permute-start | bytes 1179656 | tf_op jit(solution)/shard_map/ppermute | solution.py:70
  128.6 47.9 %collective-permute-start.17 = (bf16[128,1536]{1,0:T(8,128)(2,1)}, bf16[128,1536]{1,0:T(8,128)(2,1)}, u32[]{:S(2)}, u32[]{:S(2)}) collective-permute-start(bf16[128,1536]{1,0:T(8,128)(2,1)} %collective-permute-done.13), channel_id=1, source_target_pairs={{0,1},{1,0},{2,3},{3,2},{4,5},{5,4},{6,7},{7,6},{8,9},{9,8},{10,11... | collective-permute-start | bytes 1179656 | tf_op jit(solution)/shard_map/ppermute | solution.py:70
  139.3 115.1 %collective-permute-start.33 = (bf16[128,1536]{1,0:T(8,128)(2,1)}, bf16[128,1536]{1,0:T(8,128)(2,1)}, u32[]{:S(2)}, u32[]{:S(2)}) collective-permute-start(bf16[128,1536]{1,0:T(8,128)(2,1)} %collective-permute-done.29), channel_id=1, source_target_pairs={{0,1},{1,0},{2,3},{3,2},{4,5},{5,4},{6,7},{7,6},{8,9},{9,8},{10,11... | collective-permute-start | bytes 1179656 | tf_op jit(solution)/shard_map/ppermute | solution.py:70
  141.5 114.7 %collective-permute-start.34 = (bf16[128,1536]{1,0:T(8,128)(2,1)}, bf16[128,1536]{1,0:T(8,128)(2,1)}, u32[]{:S(2)}, u32[]{:S(2)}) collective-permute-start(bf16[128,1536]{1,0:T(8,128)(2,1)} %collective-permute-done.30), channel_id=1, source_target_pairs={{0,1},{1,0},{2,3},{3,2},{4,5},{5,4},{6,7},{7,6},{8,9},{9,8},{10,11... | collective-permute-start | bytes 1179656 | tf_op jit(solution)/shard_map/ppermute | solution.py:70
  142.4 115.6 %collective-permute-start.35 = (bf16[128,1536]{1,0:T(8,128)(2,1)}, bf16[128,1536]{1,0:T(8,128)(2,1)}, u32[]{:S(2)}, u32[]{:S(2)}) collective-permute-start(bf16[128,1536]{1,0:T(8,128)(2,1)} %collective-permute-done.31), channel_id=1, source_target_pairs={{0,1},{1,0},{2,3},{3,2},{4,5},{5,4},{6,7},{7,6},{8,9},{9,8},{10,11... | collective-permute-start | bytes 1179656 | tf_op jit(solution)/shard_map/ppermute | solution.py:70
  174.0 10.2 %collective-permute-start = (bf16[128,1536]{1,0:T(8,128)(2,1)S(1)}, bf16[128,1536]{1,0:T(8,128)(2,1)S(1)}, u32[]{:S(2)}, u32[]{:S(2)}) collective-permute-start(bf16[128,1536]{1,0:T(8,128)(2,1)S(1)} %get-tuple-element.18), channel_id=1, source_target_pairs={{0,2},{1,3},{2,4},{3,5},{4,6},{5,7},{6,0},{7,1},{8,10},{9,11},{10,... | collective-permute-start | bytes 1179656 | tf_op jit(solution)/shard_map/ppermute | solution.py:67
  176.5 24.4 %collective-permute-start.1 = (bf16[128,1536]{1,0:T(8,128)(2,1)S(1)}, bf16[128,1536]{1,0:T(8,128)(2,1)S(1)}, u32[]{:S(2)}, u32[]{:S(2)}) collective-permute-start(bf16[128,1536]{1,0:T(8,128)(2,1)S(1)} %get-tuple-element.18), channel_id=1, source_target_pairs={{0,4},{1,5},{2,6},{3,7},{4,0},{5,1},{6,2},{7,3},{8,12},{9,13},{10,... | collective-permute-start | bytes 1179656 | tf_op jit(solution)/shard_map/ppermute | solution.py:67
  184.2 21.0 %collective-permute-start.2 = (bf16[128,1536]{1,0:T(8,128)(2,1)S(1)}, bf16[128,1536]{1,0:T(8,128)(2,1)S(1)}, u32[]{:S(2)}, u32[]{:S(2)}) collective-permute-start(bf16[128,1536]{1,0:T(8,128)(2,1)S(1)} %get-tuple-element.18), channel_id=1, source_target_pairs={{0,6},{1,7},{2,0},{3,1},{4,2},{5,3},{6,4},{7,5},{8,14},{9,15},{10,... | collective-permute-start | bytes 1179656 | tf_op jit(solution)/shard_map/ppermute | solution.py:67
  200.9 11.9 %collective-permute-start.3 = (bf16[128,1536]{1,0:T(8,128)(2,1)S(1)}, bf16[128,1536]{1,0:T(8,128)(2,1)S(1)}, u32[]{:S(2)}, u32[]{:S(2)}) collective-permute-start(bf16[128,1536]{1,0:T(8,128)(2,1)S(1)} %get-tuple-element.18), channel_id=1, source_target_pairs={{0,1},{1,0},{2,3},{3,2},{4,5},{5,4},{6,7},{7,6},{8,9},{9,8},{10,11... | collective-permute-start | bytes 1179656 | tf_op jit(solution)/shard_map/ppermute | solution.py:70
  205.2 8.9 %collective-permute-start.4 = (bf16[128,1536]{1,0:T(8,128)(2,1)S(1)}, bf16[128,1536]{1,0:T(8,128)(2,1)S(1)}, u32[]{:S(2)}, u32[]{:S(2)}) collective-permute-start(bf16[128,1536]{1,0:T(8,128)(2,1)S(1)} %collective-permute-done), channel_id=1, source_target_pairs={{0,1},{1,0},{2,3},{3,2},{4,5},{5,4},{6,7},{7,6},{8,9},{9,8},{10,11... | collective-permute-start | bytes 1179656 | tf_op jit(solution)/shard_map/ppermute | solution.py:70
  259.9 3.8 collective-permute-start.36
  263.8 16.8 %collective-permute-start.37 = (bf16[2,128,448]{1,2,0:T(8,128)(2,1)S(1)}, bf16[2,128,448]{1,2,0:T(8,128)(2,1)S(1)}, u32[]{:S(2)}, u32[]{:S(2)}) collective-permute-start(bf16[2,128,448]{1,2,0:T(8,128)(2,1)S(1)} %get-tuple-element.39), channel_id=1, source_target_pairs={{0,2},{1,3},{2,4},{3,5},{4,6},{5,7},{6,0},{7,1},{8,10},{9,11},{10,... | collective-permute-start | bytes 688136 | tf_op jit(solution)/shard_map/ppermute | solution.py:67
  263.8 16.8 %collective-permute-start.38 = (bf16[2,128,448]{1,2,0:T(8,128)(2,1)S(1)}, bf16[2,128,448]{1,2,0:T(8,128)(2,1)S(1)}, u32[]{:S(2)}, u32[]{:S(2)}) collective-permute-start(bf16[2,128,448]{1,2,0:T(8,128)(2,1)S(1)} %get-tuple-element.40), channel_id=1, source_target_pairs={{0,4},{1,5},{2,6},{3,7},{4,0},{5,1},{6,2},{7,3},{8,12},{9,13},{10,... | collective-permute-start | bytes 688136 | tf_op jit(solution)/shard_map/ppermute | solution.py:67
  264.2 36.7 %collective-permute-start.39 = (bf16[2,128,448]{1,2,0:T(8,128)(2,1)S(1)}, bf16[2,128,448]{1,2,0:T(8,128)(2,1)S(1)}, u32[]{:S(2)}, u32[]{:S(2)}) collective-permute-start(bf16[2,128,448]{1,2,0:T(8,128)(2,1)S(1)} %get-tuple-element.37), channel_id=1, source_target_pairs={{0,6},{1,7},{2,0},{3,1},{4,2},{5,3},{6,4},{7,5},{8,14},{9,15},{10,... | collective-permute-start | bytes 688136 | tf_op jit(solution)/shard_map/ppermute | solution.py:67
  292.6 8.5 %collective-permute-start.18 = (bf16[4,128,1536]{2,1,0:T(8,128)(2,1)S(1)}, bf16[4,128,1536]{2,1,0:T(8,128)(2,1)S(1)}, u32[]{:S(2)}, u32[]{:S(2)}) collective-permute-start(bf16[4,128,1536]{2,1,0:T(8,128)(2,1)S(1)} %bitcast.375), channel_id=1, source_target_pairs={{0,1},{1,0},{2,3},{3,2},{4,5},{5,4},{6,7},{7,6},{8,9},{9,8},{10,11... | collective-permute-start | bytes 4718600 | tf_op jit(solution)/shard_map/ppermute | solution.py:70
  299.4 8.8 %collective-permute-start.7 = (bf16[4,128,1536]{2,1,0:T(8,128)(2,1)S(1)}, bf16[4,128,1536]{2,1,0:T(8,128)(2,1)S(1)}, u32[]{:S(2)}, u32[]{:S(2)}) collective-permute-start(bf16[4,128,1536]{2,1,0:T(8,128)(2,1)S(1)} %bitcast.374), channel_id=1, source_target_pairs={{0,1},{1,0},{2,3},{3,2},{4,5},{5,4},{6,7},{7,6},{8,9},{9,8},{10,11... | collective-permute-start | bytes 4718600 | tf_op jit(solution)/shard_map/ppermute | solution.py:70
  301.5 15.3 %collective-permute-start.21 = (bf16[128,1536]{1,0:T(8,128)(2,1)S(1)}, bf16[128,1536]{1,0:T(8,128)(2,1)S(1)}, u32[]{:S(2)}, u32[]{:S(2)}) collective-permute-start(bf16[128,1536]{1,0:T(8,128)(2,1)S(1)} %get-tuple-element.23), channel_id=1, source_target_pairs={{0,2},{1,3},{2,4},{3,5},{4,6},{5,7},{6,0},{7,1},{8,10},{9,11},{10,... | collective-permute-start | bytes 1179656 | tf_op jit(solution)/shard_map/ppermute | solution.py:67
  307.0 25.5 %collective-permute-start.20 = (bf16[128,1536]{1,0:T(8,128)(2,1)S(1)}, bf16[128,1536]{1,0:T(8,128)(2,1)S(1)}, u32[]{:S(2)}, u32[]{:S(2)}) collective-permute-start(bf16[128,1536]{1,0:T(8,128)(2,1)S(1)} %get-tuple-element.24), channel_id=1, source_target_pairs={{0,4},{1,5},{2,6},{3,7},{4,0},{5,1},{6,2},{7,3},{8,12},{9,13},{10,... | collective-permute-start | bytes 1179656 | tf_op jit(solution)/shard_map/ppermute | solution.py:67
  307.0 50.8 %collective-permute-start.19 = (bf16[128,1536]{1,0:T(8,128)(2,1)S(1)}, bf16[128,1536]{1,0:T(8,128)(2,1)S(1)}, u32[]{:S(2)}, u32[]{:S(2)}) collective-permute-start(bf16[128,1536]{1,0:T(8,128)(2,1)S(1)} %get-tuple-element.22), channel_id=1, source_target_pairs={{0,6},{1,7},{2,0},{3,1},{4,2},{5,3},{6,4},{7,5},{8,14},{9,15},{10,... | collective-permute-start | bytes 1179656 | tf_op jit(solution)/shard_map/ppermute | solution.py:67
  309.6 176.6 %collective-permute-start.10 = (bf16[128,1536]{1,0:T(8,128)(2,1)}, bf16[128,1536]{1,0:T(8,128)(2,1)}, u32[]{:S(2)}, u32[]{:S(2)}) collective-permute-start(bf16[128,1536]{1,0:T(8,128)(2,1)} %get-tuple-element.26), channel_id=1, source_target_pairs={{0,2},{1,3},{2,4},{3,5},{4,6},{5,7},{6,0},{7,1},{8,10},{9,11},{10,... | collective-permute-start | bytes 1179656 | tf_op jit(solution)/shard_map/ppermute | solution.py:67
  311.0 175.5 %collective-permute-start.9 = (bf16[128,1536]{1,0:T(8,128)(2,1)}, bf16[128,1536]{1,0:T(8,128)(2,1)}, u32[]{:S(2)}, u32[]{:S(2)}) collective-permute-start(bf16[128,1536]{1,0:T(8,128)(2,1)} %get-tuple-element.27), channel_id=1, source_target_pairs={{0,4},{1,5},{2,6},{3,7},{4,0},{5,1},{6,2},{7,3},{8,12},{9,13},{10,... | collective-permute-start | bytes 1179656 | tf_op jit(solution)/shard_map/ppermute | solution.py:67
  384.3 7.0 %collective-permute-start.24 = (bf16[128,512]{1,0:T(8,128)(2,1)}, bf16[128,512]{1,0:T(8,128)(2,1)}, u32[]{:S(2)}, u32[]{:S(2)}) collective-permute-start(bf16[128,512]{1,0:T(8,128)(2,1)} %get-tuple-element.51), channel_id=1, source_target_pairs={{0,24},{8,16},{16,8},{24,0},{1,25},{9,17},{17,9},{25,1},{2,26},{10... | collective-permute-start | bytes 393224 | tf_op jit(solution)/shard_map/ppermute | solution.py:105
  384.3 9.4 %collective-permute-start.23 = (bf16[128,512]{1,0:T(8,128)(2,1)}, bf16[128,512]{1,0:T(8,128)(2,1)}, u32[]{:S(2)}, u32[]{:S(2)}) collective-permute-start(bf16[128,512]{1,0:T(8,128)(2,1)} %get-tuple-element.50), channel_id=1, source_target_pairs={{0,16},{8,24},{16,0},{24,8},{1,17},{9,25},{17,1},{25,9},{2,18},{10... | collective-permute-start | bytes 393224 | tf_op jit(solution)/shard_map/ppermute | solution.py:105
  386.6 8.0 %collective-permute-start.22 = (bf16[128,512]{1,0:T(8,128)(2,1)}, bf16[128,512]{1,0:T(8,128)(2,1)}, u32[]{:S(2)}, u32[]{:S(2)}) collective-permute-start(bf16[128,512]{1,0:T(8,128)(2,1)} %get-tuple-element.49), channel_id=1, source_target_pairs={{0,8},{8,0},{16,24},{24,16},{1,9},{9,1},{17,25},{25,17},{2,10},{10... | collective-permute-start | bytes 393224 | tf_op jit(solution)/shard_map/ppermute | solution.py:105
  391.3 19.8 %collective-permute-start.40 = (bf16[128,1536]{1,0:T(8,128)(2,1)}, bf16[128,1536]{1,0:T(8,128)(2,1)}, u32[]{:S(2)}, u32[]{:S(2)}) collective-permute-start(bf16[128,1536]{1,0:T(8,128)(2,1)} %copy-done.23), channel_id=1, source_target_pairs={{0,2},{1,3},{2,4},{3,5},{4,6},{5,7},{6,0},{7,1},{8,10},{9,11},{10,... | collective-permute-start | bytes 1179656 | tf_op jit(solution)/shard_map/ppermute | solution.py:67
  393.7 29.6 %collective-permute-start.41 = (bf16[128,1536]{1,0:T(8,128)(2,1)}, bf16[128,1536]{1,0:T(8,128)(2,1)}, u32[]{:S(2)}, u32[]{:S(2)}) collective-permute-start(bf16[128,1536]{1,0:T(8,128)(2,1)} %copy-done.23), channel_id=1, source_target_pairs={{0,4},{1,5},{2,6},{3,7},{4,0},{5,1},{6,2},{7,3},{8,12},{9,13},{10,... | collective-permute-start | bytes 1179656 | tf_op jit(solution)/shard_map/ppermute | solution.py:67
  394.7 29.8 %collective-permute-start.42 = (bf16[128,1536]{1,0:T(8,128)(2,1)}, bf16[128,1536]{1,0:T(8,128)(2,1)}, u32[]{:S(2)}, u32[]{:S(2)}) collective-permute-start(bf16[128,1536]{1,0:T(8,128)(2,1)} %copy-done.23), channel_id=1, source_target_pairs={{0,6},{1,7},{2,0},{3,1},{4,2},{5,3},{6,4},{7,5},{8,14},{9,15},{10,... | collective-permute-start | bytes 1179656 | tf_op jit(solution)/shard_map/ppermute | solution.py:67
  411.1 14.9 %collective-permute-start.43 = (bf16[128,1536]{1,0:T(8,128)(2,1)S(1)}, bf16[128,1536]{1,0:T(8,128)(2,1)S(1)}, u32[]{:S(2)}, u32[]{:S(2)}) collective-permute-start(bf16[128,1536]{1,0:T(8,128)(2,1)S(1)} %copy-done.24), channel_id=1, source_target_pairs={{0,1},{1,0},{2,3},{3,2},{4,5},{5,4},{6,7},{7,6},{8,9},{9,8},{10,11... | collective-permute-start | bytes 1179656 | tf_op jit(solution)/shard_map/ppermute | solution.py:70
  426.1 6.1 %collective-permute-start.45 = (bf16[128,1536]{1,0:T(8,128)(2,1)}, bf16[128,1536]{1,0:T(8,128)(2,1)S(1)}, u32[]{:S(2)}, u32[]{:S(2)}) collective-permute-start(bf16[128,1536]{1,0:T(8,128)(2,1)} %collective-permute-done.41), channel_id=1, source_target_pairs={{0,1},{1,0},{2,3},{3,2},{4,5},{5,4},{6,7},{7,6},{8,9},{9,8},{10,11... | collective-permute-start | bytes 1179656 | tf_op jit(solution)/shard_map/ppermute | solution.py:70
  426.2 10.0 %collective-permute-start.46 = (bf16[128,1536]{1,0:T(8,128)(2,1)}, bf16[128,1536]{1,0:T(8,128)(2,1)S(1)}, u32[]{:S(2)}, u32[]{:S(2)}) collective-permute-start(bf16[128,1536]{1,0:T(8,128)(2,1)} %collective-permute-done.42), channel_id=1, source_target_pairs={{0,1},{1,0},{2,3},{3,2},{4,5},{5,4},{6,7},{7,6},{8,9},{9,8},{10,11... | collective-permute-start | bytes 1179656 | tf_op jit(solution)/shard_map/ppermute | solution.py:70
  427.5 13.5 %collective-permute-start.28 = (bf16[2,144,448]{2,1,0:T(8,128)(2,1)S(1)}, bf16[2,144,448]{2,1,0:T(8,128)(2,1)S(1)}, u32[]{:S(2)}, u32[]{:S(2)}) collective-permute-start(bf16[2,144,448]{2,1,0:T(8,128)(2,1)S(1)} %get-tuple-element.34), channel_id=1, source_target_pairs={{0,6},{1,7},{2,0},{3,1},{4,2},{5,3},{6,4},{7,5},{8,14},{9,15},{10,... | collective-permute-start | bytes 774152 | tf_op jit(solution)/shard_map/ppermute | solution.py:67
  432.2 24.9 %collective-permute-start.27 = (bf16[2,144,448]{2,1,0:T(8,128)(2,1)S(1)}, bf16[2,144,448]{2,1,0:T(8,128)(2,1)S(1)}, u32[]{:S(2)}, u32[]{:S(2)}) collective-permute-start(bf16[2,144,448]{2,1,0:T(8,128)(2,1)S(1)} %get-tuple-element.33), channel_id=1, source_target_pairs={{0,4},{1,5},{2,6},{3,7},{4,0},{5,1},{6,2},{7,3},{8,12},{9,13},{10,... | collective-permute-start | bytes 774152 | tf_op jit(solution)/shard_map/ppermute | solution.py:67
  436.3 34.1 %collective-permute-start.26 = (bf16[2,144,448]{2,1,0:T(8,128)(2,1)S(1)}, bf16[2,144,448]{2,1,0:T(8,128)(2,1)S(1)}, u32[]{:S(2)}, u32[]{:S(2)}) collective-permute-start(bf16[2,144,448]{2,1,0:T(8,128)(2,1)S(1)} %get-tuple-element.32), channel_id=1, source_target_pairs={{0,2},{1,3},{2,4},{3,5},{4,6},{5,7},{6,0},{7,1},{8,10},{9,11},{10,... | collective-permute-start | bytes 774152 | tf_op jit(solution)/shard_map/ppermute | solution.py:67
  441.1 45.4 %collective-permute-start.8 = (bf16[128,1536]{1,0:T(8,128)(2,1)}, bf16[128,1536]{1,0:T(8,128)(2,1)}, u32[]{:S(2)}, u32[]{:S(2)}) collective-permute-start(bf16[128,1536]{1,0:T(8,128)(2,1)} %get-tuple-element.25), channel_id=1, source_target_pairs={{0,6},{1,7},{2,0},{3,1},{4,2},{5,3},{6,4},{7,5},{8,14},{9,15},{10,... | collective-permute-start | bytes 1179656 | tf_op jit(solution)/shard_map/ppermute | solution.py:67
  483.8 10.8 %collective-permute-start.49 = (bf16[128,1536]{1,0:T(8,128)(2,1)S(1)}, bf16[128,1536]{1,0:T(8,128)(2,1)S(1)}, u32[]{:S(2)}, u32[]{:S(2)}) collective-permute-start(bf16[128,1536]{1,0:T(8,128)(2,1)S(1)} %get-tuple-element.29), channel_id=1, source_target_pairs={{0,24},{8,16},{16,8},{24,0},{1,25},{9,17},{17,9},{25,1},{2,26},{10... | collective-permute-start | bytes 1179656 | tf_op jit(solution)/shard_map/ppermute | solution.py:105
  484.8 19.4 %collective-permute-start.48 = (bf16[128,1536]{1,0:T(8,128)(2,1)S(1)}, bf16[128,1536]{1,0:T(8,128)(2,1)S(1)}, u32[]{:S(2)}, u32[]{:S(2)}) collective-permute-start(bf16[128,1536]{1,0:T(8,128)(2,1)S(1)} %get-tuple-element.30), channel_id=1, source_target_pairs={{0,16},{8,24},{16,0},{24,8},{1,17},{9,25},{17,1},{25,9},{2,18},{10... | collective-permute-start | bytes 1179656 | tf_op jit(solution)/shard_map/ppermute | solution.py:105
  486.2 18.0 %collective-permute-start.47 = (bf16[128,1536]{1,0:T(8,128)(2,1)S(1)}, bf16[128,1536]{1,0:T(8,128)(2,1)S(1)}, u32[]{:S(2)}, u32[]{:S(2)}) collective-permute-start(bf16[128,1536]{1,0:T(8,128)(2,1)S(1)} %get-tuple-element.28), channel_id=1, source_target_pairs={{0,8},{8,0},{16,24},{24,16},{1,9},{9,1},{17,25},{25,17},{2,10},{10... | collective-permute-start | bytes 1179656 | tf_op jit(solution)/shard_map/ppermute | solution.py:105
  (58 other events, 891.3 us)
Sparse Core Ops, SparseCore 0:
  11.5 126.3 all-gather.2
  254.5 101.8 reduce-scatter.3
